TPU v7x, 32 devices: a whole 2x2x4 slice. The times are simulated.
32 devices in a mesh: section: 4 (over y, x), dp: 8 (over z, core).
Axes of the slice: x: 2, y: 2, z: 4, core: 2. Of those that a mesh axis runs over, the one named last changes fastest.
Arguments:
- inputs: bfloat16 [4, 4096, 768], P('section', 'dp'), may hold values from -6 to 6
- cotangent: bfloat16 [4, 4096, 768], P('section', 'dp'), may hold values from -6 to 6
- wide: bfloat16 [4, 768, 3072], P('section'), may hold values from -0.21875 to 0.21875
- down: bfloat16 [4, 3072, 768], P('section'), may hold values from -0.109375 to 0.109375
- vectors: float32 [4, 7, 768], P('section'), may hold values from -1.6 to 2.6
- seg_counts: int32 [8, 4, 4], P('dp'), may hold values from 0 to 4, as said below
Outputs:
- layer_out: bfloat16 [4, 4096, 768], P('section', 'dp')
- input_grad: bfloat16 [4, 4096, 768], P('section', 'dp')
- wide_grad: float32 [4, 768, 3072], P('section')
- down_grad: float32 [4, 3072, 768], P('section')
- vectors_grad: float32 [4, 7, 768], P('section')
Inputs may be any that keep to these rules, and one draw needn't show every extreme that they name: seg_counts[r, m] are the segment counts of the documents of micro-batch m on dp index r, in order; they sum to 4, trailing ones may be 0, and on every dp index one micro-batch holds a single document of 4 segments.
All inputs are finite; a program needn't handle non-finite values.
Results may differ from a plain program's by a relative error of at most 0.009.
Values may be sent and summed in bfloat16 or wider, within the bound.
No kernel may reach another device: no remote copies, remote signals or barrier semaphores. Data moves between devices by JAX's collectives and lax.ppermute only.
A program may use at most 256 MiB of HBM per device.

v0:
```python
from functools import partial

import jax
import jax.numpy as jnp
from jax import lax
from jax.sharding import PartitionSpec as P

HEADS = 12
SEG = 128
SEGS = 4


EPSILON = 1e-05
SCORE_SCALE = 0.125
MASKED = -1e30
PRECISE = lax.Precision.HIGHEST


def shifted(shard, axis, by):
    devices = lax.axis_size(axis)
    pairs = [(i, i + by) for i in range(devices) if 0 <= i + by < devices]
    return lax.ppermute(shard, axis, pairs)


def norm_rows(values, gain_row, shift_row):
    center = values - jnp.mean(values, -1, keepdims=True)
    spread = jnp.mean(center * center, -1, keepdims=True)
    return center * lax.rsqrt(spread + EPSILON) * gain_row + shift_row


def product(left_side, right_side):
    return jnp.dot(left_side, right_side, preferred_element_type=jnp.float32)


def segment_layout(counts):
    places = jnp.arange(SEGS, dtype=jnp.int32)
    doc_ends = jnp.cumsum(counts)
    doc_index = jnp.sum((places[:, None] >= doc_ends[None, :]).astype(jnp.int32), 1)
    starts = doc_ends - counts
    doc_slots = jnp.arange(counts.shape[0], dtype=jnp.int32)
    doc_first = jnp.sum(jnp.where(doc_index[:, None] == doc_slots[None, :], starts[None, :], 0), 1)
    position = places - doc_first
    same_doc = doc_index[:, None] == doc_index[None, :]
    onehot = (position[:, None] == places[None, :]).astype(jnp.float32)
    return (same_doc, onehot)


def softmax_parts(query_rows, key_rows, allowed):
    scores = (
        jnp.einsum("glhe,gmhe->ghlm", query_rows, key_rows, preferred_element_type=jnp.float32)
        * SCORE_SCALE
    )
    scores = jnp.where(allowed[:, None], scores, MASKED)
    maxima = jnp.max(scores, -1, keepdims=True)
    powers = jnp.exp(scores - maxima)
    return powers / jnp.sum(powers, -1, keepdims=True)


def split_heads(triple, features, groups, length):
    query_rows = triple[:, :features].reshape(groups, length, HEADS, -1)
    key_rows = triple[:, features : 2 * features].reshape(groups, length, HEADS, -1)
    value_rows = triple[:, 2 * features : 3 * features].reshape(groups, length, HEADS, -1)
    return (query_rows, key_rows, value_rows)


def attention_forward(values, wide_w, vector, allowed, groups, length):
    features = values.shape[1]
    normed = norm_rows(values, vector[0], vector[1]).astype(jnp.bfloat16)
    triple = product(normed, wide_w[:, : 3 * features]).astype(jnp.bfloat16)
    query_rows, key_rows, value_rows = split_heads(triple, features, groups, length)
    weights = softmax_parts(query_rows, key_rows, allowed).astype(jnp.bfloat16)
    mixture = jnp.einsum("ghlm,gmhe->glhe", weights, value_rows, preferred_element_type=jnp.float32)
    mixture = mixture.astype(jnp.bfloat16).reshape(groups * length, features)
    output = values + product(mixture, wide_w[:, 3 * features :]) + vector[2]
    internals = jnp.concatenate([triple, mixture], 1).astype(jnp.float32)
    return (output, internals)


def attention_backward(values, internals, grad_out, wide_w, vector, allowed, groups, length):
    features = values.shape[1]
    triple = internals[:, : 3 * features].astype(jnp.bfloat16)
    mixture = internals[:, 3 * features :].astype(jnp.bfloat16)
    query_rows, key_rows, value_rows = split_heads(triple, features, groups, length)
    probs = softmax_parts(query_rows, key_rows, allowed)
    weights = probs.astype(jnp.bfloat16)
    grad_branch = grad_out.astype(jnp.bfloat16)
    grad_proj = product(mixture.T, grad_branch)
    grad_mix = product(grad_branch, wide_w[:, 3 * features :].T).astype(jnp.bfloat16)
    grad_mix = grad_mix.reshape(groups, length, HEADS, -1)
    grad_value = jnp.einsum(
        "ghlm,glhe->gmhe", weights, grad_mix, preferred_element_type=jnp.float32
    )
    grad_probs = jnp.einsum(
        "glhe,gmhe->ghlm", grad_mix, value_rows, preferred_element_type=jnp.float32
    )
    grad_scores = probs * (grad_probs - jnp.sum(grad_probs * probs, -1, keepdims=True))
    grad_scores = grad_scores.astype(jnp.bfloat16)
    grad_query = (
        jnp.einsum("ghlm,gmhe->glhe", grad_scores, key_rows, preferred_element_type=jnp.float32)
        * SCORE_SCALE
    )
    grad_key = (
        jnp.einsum("ghlm,glhe->gmhe", grad_scores, query_rows, preferred_element_type=jnp.float32)
        * SCORE_SCALE
    )
    row_total = groups * length
    grad_triple = jnp.concatenate(
        [
            grad_query.reshape(row_total, features),
            grad_key.reshape(row_total, features),
            grad_value.reshape(row_total, features),
        ],
        1,
    ).astype(jnp.bfloat16)
    normed, norm_pull = jax.vjp(norm_rows, values, vector[0], vector[1])
    grad_qkv = product(normed.astype(jnp.bfloat16).T, grad_triple)
    grad_normed = product(grad_triple, wide_w[:, : 3 * features].T)
    grad_rows, grad_gain, grad_shift = norm_pull(grad_normed)
    grad_wide = jnp.concatenate([grad_qkv, grad_proj], 1)
    small_rows = jnp.stack([grad_gain, grad_shift, jnp.sum(grad_out, 0)])
    return (grad_out + grad_rows, grad_wide, small_rows)


def mlp_forward(values, wide_w, down_w, vector):
    normed = norm_rows(values, vector[0], vector[1]).astype(jnp.bfloat16)
    hidden = product(normed, wide_w)
    active = jax.nn.gelu(hidden, approximate=True).astype(jnp.bfloat16)
    return (values + product(active, down_w) + vector[2], hidden)


def mlp_backward(values, hidden, grad_out, wide_w, down_w, vector):
    active, gelu_pull = jax.vjp(partial(jax.nn.gelu, approximate=True), hidden)
    grad_branch = grad_out.astype(jnp.bfloat16)
    grad_down = product(active.astype(jnp.bfloat16).T, grad_branch)
    grad_active = product(grad_branch, down_w.T)
    grad_hidden = gelu_pull(grad_active)[0].astype(jnp.bfloat16)
    normed, norm_pull = jax.vjp(norm_rows, values, vector[0], vector[1])
    grad_up = product(normed.astype(jnp.bfloat16).T, grad_hidden)
    grad_normed = product(grad_hidden, wide_w.T)
    grad_rows, grad_gain, grad_shift = norm_pull(grad_normed)
    small_rows = jnp.stack([grad_gain, grad_shift, jnp.sum(grad_out, 0)])
    return (grad_out + grad_rows, grad_up, grad_down, small_rows)


def pad_rows(small_rows, row_count):
    return (
        jnp.zeros((row_count, small_rows.shape[1]), small_rows.dtype)
        .at[: small_rows.shape[0]]
        .set(small_rows)
    )


def put_slot(buffer, item, batch_slot, running):
    previous = lax.dynamic_index_in_dim(buffer, batch_slot, 0, keepdims=False)
    return lax.dynamic_update_index_in_dim(
        buffer, jnp.where(running, item, previous), batch_slot, 0
    )


def local(inputs, cotangent, wide, down, vectors, seg_counts):
    sections = lax.axis_size("section")
    section_index = lax.axis_index("section")
    row_count = inputs.shape[1]
    features = inputs.shape[2]
    hidden_width = wide.shape[2]
    seg_count = row_count // SEG
    micro_count = inputs.shape[0] * sections
    wide_w = wide[0]
    down_w = down[0]
    vector = vectors[0]
    batch_counts = seg_counts[0]
    every_input, every_cot = (
        lax.all_gather(inputs, "section", axis=0, tiled=True),
        lax.all_gather(cotangent, "section", axis=0, tiled=True),
    )
    allowed = jnp.ones((1, SEG, SEG), bool)
    zero_pos = jnp.zeros((seg_count, features), jnp.float32)

    def seg_attention(values, same_doc, onehot):
        return attention_forward(values, wide_w, vector, allowed, seg_count, SEG)

    def seg_mlp(values, same_doc, onehot):
        return mlp_forward(values, wide_w, down_w, vector)

    def cross_attention(values, same_doc, onehot):
        seg_grid = values.reshape(seg_count, SEG, features)
        lifted = seg_grid[:, 0] + jnp.dot(onehot, vector[3:], precision=PRECISE)
        output, internals = attention_forward(lifted, wide_w, vector, same_doc[None], 1, seg_count)
        return (
            seg_grid.at[:, 0].set(output).reshape(row_count, features),
            pad_rows(internals, row_count),
        )

    def cross_mlp(values, same_doc, onehot):
        seg_grid = values.reshape(seg_count, SEG, features)
        output, hidden = mlp_forward(seg_grid[:, 0], wide_w, down_w, vector)
        return (
            seg_grid.at[:, 0].set(output).reshape(row_count, features),
            pad_rows(hidden, row_count),
        )

    def seg_attention_back(values, internals, gradient, same_doc, onehot, sums):
        grad_rows, grad_wide, small_rows = attention_backward(
            values, internals, gradient, wide_w, vector, allowed, seg_count, SEG
        )
        return (
            grad_rows,
            sums[0] + grad_wide,
            sums[1],
            sums[2] + jnp.concatenate([small_rows, zero_pos], 0),
        )

    def seg_mlp_back(values, internals, gradient, same_doc, onehot, sums):
        grad_rows, grad_up, grad_down, small_rows = mlp_backward(
            values, internals, gradient, wide_w, down_w, vector
        )
        return (
            grad_rows,
            sums[0] + grad_up,
            sums[1] + grad_down,
            sums[2] + jnp.concatenate([small_rows, zero_pos], 0),
        )

    def cross_attention_back(values, internals, gradient, same_doc, onehot, sums):
        seg_grid = values.reshape(seg_count, SEG, features)
        lifted = seg_grid[:, 0] + jnp.dot(onehot, vector[3:], precision=PRECISE)
        grad_grid = gradient.reshape(seg_count, SEG, features)
        grad_lifted, grad_wide, small_rows = attention_backward(
            lifted,
            internals[:seg_count],
            grad_grid[:, 0],
            wide_w,
            vector,
            same_doc[None],
            1,
            seg_count,
        )
        grad_pos = jnp.dot(onehot.T, grad_lifted, precision=PRECISE)
        grad_rows = grad_grid.at[:, 0].set(grad_lifted).reshape(row_count, features)
        return (
            grad_rows,
            sums[0] + grad_wide,
            sums[1],
            sums[2] + jnp.concatenate([small_rows, grad_pos], 0),
        )

    def cross_mlp_back(values, internals, gradient, same_doc, onehot, sums):
        seg_grid = values.reshape(seg_count, SEG, features)
        grad_grid = gradient.reshape(seg_count, SEG, features)
        grad_heads, grad_up, grad_down, small_rows = mlp_backward(
            seg_grid[:, 0], internals[:seg_count], grad_grid[:, 0], wide_w, down_w, vector
        )
        grad_rows = grad_grid.at[:, 0].set(grad_heads).reshape(row_count, features)
        return (
            grad_rows,
            sums[0] + grad_up,
            sums[1] + grad_down,
            sums[2] + jnp.concatenate([small_rows, zero_pos], 0),
        )

    forward_list = [seg_attention, seg_mlp, cross_attention, cross_mlp]
    backward_list = [seg_attention_back, seg_mlp_back, cross_attention_back, cross_mlp_back]

    def run_forward(operands):
        return lax.switch(section_index, forward_list, *operands)

    def skip_forward(operands):
        return (
            jnp.zeros((row_count, features), jnp.float32),
            jnp.zeros((row_count, hidden_width), jnp.float32),
        )

    def run_backward(operands):
        return lax.switch(section_index, backward_list, *operands)

    def skip_backward(operands):
        sums = operands[5]
        return (jnp.zeros((row_count, features), jnp.float32), sums[0], sums[1], sums[2])

    received = jnp.zeros((row_count, features), jnp.bfloat16)
    kept_rows = jnp.zeros((micro_count, row_count, features), jnp.bfloat16)
    kept_inner = jnp.zeros((micro_count, row_count, hidden_width), jnp.float32)
    outputs_all = jnp.zeros((micro_count, row_count, features), jnp.bfloat16)
    grads_all = jnp.zeros((micro_count, row_count, features), jnp.bfloat16)
    for instant in range(micro_count + sections - 1):
        batch_index = instant - section_index
        running = (batch_index >= 0) & (batch_index < micro_count)
        batch_slot = jnp.clip(batch_index, 0, micro_count - 1)
        fresh_rows = lax.dynamic_index_in_dim(every_input, batch_slot, 0, keepdims=False)
        entering = jnp.where(section_index == 0, fresh_rows, received)
        same_doc, onehot = segment_layout(
            lax.dynamic_index_in_dim(batch_counts, batch_slot, 0, keepdims=False)
        )
        result, internals = lax.cond(
            running, run_forward, skip_forward, (entering.astype(jnp.float32), same_doc, onehot)
        )
        kept_rows = put_slot(kept_rows, entering, batch_slot, running)
        kept_inner = put_slot(kept_inner, internals, batch_slot, running)
        leaving = result.astype(jnp.bfloat16)
        outputs_all = put_slot(
            outputs_all, leaving, batch_slot, running & (section_index == sections - 1)
        )
        received = shifted(leaving, "section", 1)
    grad_received = jnp.zeros((row_count, features), jnp.bfloat16)
    sum_wide = jnp.zeros(wide_w.shape, jnp.float32)
    sum_down = jnp.zeros(down_w.shape, jnp.float32)
    sum_vector = jnp.zeros(vector.shape, jnp.float32)
    for instant in range(micro_count + sections - 1):
        batch_index = instant - (sections - 1 - section_index)
        running = (batch_index >= 0) & (batch_index < micro_count)
        batch_slot = jnp.clip(batch_index, 0, micro_count - 1)
        entering = lax.dynamic_index_in_dim(kept_rows, batch_slot, 0, keepdims=False).astype(
            jnp.float32
        )
        fresh_cot = lax.dynamic_index_in_dim(every_cot, batch_slot, 0, keepdims=False)
        gradient = jnp.where(section_index == sections - 1, fresh_cot, grad_received).astype(
            jnp.float32
        )
        same_doc, onehot = segment_layout(
            lax.dynamic_index_in_dim(batch_counts, batch_slot, 0, keepdims=False)
        )
        internals = lax.dynamic_index_in_dim(kept_inner, batch_slot, 0, keepdims=False)
        gradients = lax.cond(
            running,
            run_backward,
            skip_backward,
            (entering, internals, gradient, same_doc, onehot, (sum_wide, sum_down, sum_vector)),
        )
        sum_wide = gradients[1]
        sum_down = gradients[2]
        sum_vector = gradients[3]
        leaving = gradients[0].astype(jnp.bfloat16)
        grads_all = put_slot(grads_all, leaving, batch_slot, running & (section_index == 0))
        grad_received = shifted(leaving, "section", -1)
    out_sum, grad_sum = (
        lax.psum_scatter(
            outputs_all.astype(jnp.float32).astype(jnp.bfloat16),
            "section",
            scatter_dimension=0,
            tiled=True,
        ).astype(jnp.float32),
        lax.psum_scatter(
            grads_all.astype(jnp.float32).astype(jnp.bfloat16),
            "section",
            scatter_dimension=0,
            tiled=True,
        ).astype(jnp.float32),
    )
    layer_out = out_sum.astype(jnp.bfloat16)
    input_grad = grad_sum.astype(jnp.bfloat16)
    total_wide, total_down, total_vector = lax.psum((sum_wide, sum_down, sum_vector), "dp")
    return (layer_out, input_grad, total_wide[None], total_down[None], total_vector[None])


def solution(mesh):
    return jax.shard_map(
        local,
        mesh=mesh,
        in_specs=(
            P("section", "dp", None),
            P("section", "dp", None),
            P("section", None, None),
            P("section", None, None),
            P("section", None, None),
            P("dp", None, None),
        ),
        out_specs=(
            P("section", "dp", None),
            P("section", "dp", None),
            P("section", None, None),
            P("section", None, None),
            P("section", None, None),
        ),
        check_vma=False,
    )
```

profile of v0, /device:TPU:3, one launch (start us, length us, event | category | flops | bytes accessed | tf_op | source)
XLA Modules:
  0.0 1418.4 jit_solution(16417034809583811962)
XLA Ops:
  23.6 31.5 %all-gather.3.cloned.1.call-done = bf16[4,512,768]{2,1,0:T(8,128)(2,1)} async-done(((bf16[1,512,768]{2,1,0:T(8,128)(2,1)}), bf16[4,512,768]{2,1,0:T(8,128)(2,1)}) %all-gather.3.cloned.1.call-update) | async-done | bytes 3145744 | tf_op jit(solution)/shard_map/all_gather | solution.py:173
  58.4 8.3 conditional.84
  69.8 11.5 broadcast_in_dim.945
  95.0 25.6 %collective-permute-done = bf16[512,768]{1,0:T(8,128)(2,1)S(1)} collective-permute-done((bf16[512,768]{1,0:T(8,128)(2,1)}, bf16[512,768]{1,0:T(8,128)(2,1)S(1)}, u32[]{:S(2)}, u32[]{:S(2)}) %collective-permute-start) | collective-permute-done | bytes 786464 | tf_op jit(solution)/shard_map/ppermute | solution.py:22
  122.1 22.8 %conditional.85 = ((f32[512,3072]{1,0:T(8,128)}, bf16[512,768]{1,0:T(8,128)(2,1)})) conditional(s32[]{:T(128)} %convert_element_type.1426, () %tuple.738, (s32[]{:T(128)}, f32[512,768]{1,0:T(8,128)S(1)}, f32[7,768]{1,0:T(8,128)S(1)}, bf16[768,3072]{1,0:T(8,128)(2,1)}, bf16[3072,768]{1,0:T(8,128)(2,1)}, /*index=5*/f32[4,4]{1,0:T(4,128)S(1)}, ...), branch_computations={%region_24.25_spmd, %region_25.42_spmd} | conditional | flops 4850713088 | bytes 68514984 | solution.py:294
  122.2 19.7 %conditional.29 = (f32[512,3072]{1,0:T(8,128)}, bf16[512,768]{1,0:T(8,128)(2,1)}) conditional(s32[]{:T(128)} %clamp.43, (f32[512,768]{1,0:T(8,128)S(1)}, f32[7,768]{1,0:T(8,128)S(1)}, bf16[768,3072]{1,0:T(8,128)(2,1)}) %tuple.594, (f32[512,768]{1,0:T(8,128)S(1)}, f32[7,768]{1,0:T(8,128)S(1)}, ...), branch_computations={%region_26.30_spmd, %region_31.33_spmd, %region_34.38_spmd, %regio... | conditional | flops 4850713088 | bytes 68514864
  146.9 9.1 bitcast_dynamic-update-slice_fusion.26
  168.7 19.9 %collective-permute-done.1 = bf16[512,768]{1,0:T(8,128)(2,1)S(1)} collective-permute-done((bf16[512,768]{1,0:T(8,128)(2,1)}, bf16[512,768]{1,0:T(8,128)(2,1)S(1)}, u32[]{:S(2)}, u32[]{:S(2)}) %collective-permute-start.1) | collective-permute-done | bytes 786464 | tf_op jit(solution)/shard_map/ppermute | solution.py:22
  189.5 28.5 %conditional.86 = ((f32[512,3072]{1,0:T(8,128)}, bf16[512,768]{1,0:T(8,128)(2,1)})) conditional(s32[]{:T(128)} %convert_element_type.1430, () %tuple.740, (s32[]{:T(128)}, f32[512,768]{1,0:T(8,128)S(1)}, f32[7,768]{1,0:T(8,128)S(1)}, bf16[768,3072]{1,0:T(8,128)(2,1)}, bf16[3072,768]{1,0:T(8,128)(2,1)}, /*index=5*/f32[4,4]{1,0:T(4,128)S(1)}, ...), branch_computations={%region_45.46_spmd, %region_46.63_spmd} | conditional | flops 4850713088 | bytes 68514984 | solution.py:294
  189.5 20.2 %conditional.30 = (f32[512,3072]{1,0:T(8,128)}, bf16[512,768]{1,0:T(8,128)(2,1)}) conditional(s32[]{:T(128)} %clamp.44, (f32[512,768]{1,0:T(8,128)S(1)}, f32[7,768]{1,0:T(8,128)S(1)}, bf16[768,3072]{1,0:T(8,128)(2,1)}) %tuple.603, (f32[512,768]{1,0:T(8,128)S(1)}, f32[7,768]{1,0:T(8,128)S(1)}, ...), branch_computations={%region_47.51_spmd, %region_52.54_spmd, %region_55.59_spmd, %regio... | conditional | flops 4850713088 | bytes 68514864
  220.0 9.0 bitcast_dynamic-update-slice_fusion.25
  241.7 16.4 %collective-permute-done.2 = bf16[512,768]{1,0:T(8,128)(2,1)S(1)} collective-permute-done((bf16[512,768]{1,0:T(8,128)(2,1)}, bf16[512,768]{1,0:T(8,128)(2,1)S(1)}, u32[]{:S(2)}, u32[]{:S(2)}) %collective-permute-start.2) | collective-permute-done | bytes 786464 | tf_op jit(solution)/shard_map/ppermute | solution.py:22
  259.0 15.8 %conditional.87 = ((f32[512,3072]{1,0:T(8,128)}, bf16[512,768]{1,0:T(8,128)(2,1)})) conditional(s32[]{:T(128)} %convert_element_type.1434, () %tuple.742, (s32[]{:T(128)}, f32[512,768]{1,0:T(8,128)S(1)}, f32[7,768]{1,0:T(8,128)S(1)}, bf16[768,3072]{1,0:T(8,128)(2,1)}, bf16[3072,768]{1,0:T(8,128)(2,1)}, /*index=5*/f32[4,4]{1,0:T(4,128)S(1)}, ...), branch_computations={%region_66.67_spmd, %region_67.84_spmd} | conditional | flops 4850713088 | bytes 68514984 | solution.py:294
  259.0 15.8 %conditional.31 = (f32[512,3072]{1,0:T(8,128)}, bf16[512,768]{1,0:T(8,128)(2,1)}) conditional(s32[]{:T(128)} %clamp.45, (f32[512,768]{1,0:T(8,128)S(1)}, f32[7,768]{1,0:T(8,128)S(1)}, bf16[768,3072]{1,0:T(8,128)(2,1)}) %tuple.612, (f32[512,768]{1,0:T(8,128)S(1)}, f32[7,768]{1,0:T(8,128)S(1)}, ...), branch_computations={%region_68.72_spmd, %region_73.75_spmd, %region_76.80_spmd, %regio... | conditional | flops 4850713088 | bytes 68514864
  276.8 9.1 bitcast_dynamic-update-slice_fusion.24
  298.6 22.1 %collective-permute-done.3 = bf16[512,768]{1,0:T(8,128)(2,1)S(1)} collective-permute-done((bf16[512,768]{1,0:T(8,128)(2,1)}, bf16[512,768]{1,0:T(8,128)(2,1)S(1)}, u32[]{:S(2)}, u32[]{:S(2)}) %collective-permute-start.3) | collective-permute-done | bytes 786464 | tf_op jit(solution)/shard_map/ppermute | solution.py:22
  321.7 23.0 %conditional.88 = ((f32[512,3072]{1,0:T(8,128)}, bf16[512,768]{1,0:T(8,128)(2,1)})) conditional(s32[]{:T(128)} %convert_element_type.1438, () %tuple.744, (s32[]{:T(128)}, f32[512,768]{1,0:T(8,128)S(1)}, f32[7,768]{1,0:T(8,128)S(1)}, bf16[768,3072]{1,0:T(8,128)(2,1)}, bf16[3072,768]{1,0:T(8,128)(2,1)}, /*index=5*/f32[4,4]{1,0:T(4,128)S(1)}, ...), branch_computations={%region_87.88_spmd, %region_88.105_spmd} | conditional | flops 4850713088 | bytes 68514984 | solution.py:294
  321.7 20.0 %conditional.32 = (f32[512,3072]{1,0:T(8,128)}, bf16[512,768]{1,0:T(8,128)(2,1)}) conditional(s32[]{:T(128)} %clamp.46, (f32[512,768]{1,0:T(8,128)S(1)}, f32[7,768]{1,0:T(8,128)S(1)}, bf16[768,3072]{1,0:T(8,128)(2,1)}) %tuple.621, (f32[512,768]{1,0:T(8,128)S(1)}, f32[7,768]{1,0:T(8,128)S(1)}, ...), branch_computations={%region_89.93_spmd, %region_94.96_spmd, %region_97.101_spmd, %regi... | conditional | flops 4850713088 | bytes 68514864
  346.6 9.0 bitcast_dynamic-update-slice_fusion.23
  369.3 13.3 conditional.89
  403.5 11.3 conditional.90
  425.6 16.7 %conditional.98 = ((f32[768,3072]{1,0:T(8,128)}, f32[3072,768]{1,0:T(8,128)}, f32[7,768]{1,0:T(8,128)}, bf16[512,768]{1,0:T(8,128)(2,1)})) conditional(s32[]{:T(128)} %convert_element_type.1450, () %tuple.750, (s32[]{:T(128)}, f32[4,512,3072]{2,1,0:T(8,128)}, s32[]{:T(128)}, bf16[4,512,768]{2,1,0:T(8,128)(2,1)}, ...), branch_computations={%region_151.152_spmd, %region_152.191_spmd.clone.clone} | conditional | flops 9722281984 | bytes 196883968 | solution.py:323
  449.2 13.2 collective-permute-done.6
  472.0 60.9 %collective-permute-done.7 = bf16[512,768]{1,0:T(8,128)(2,1)S(1)} collective-permute-done((bf16[512,768]{1,0:T(8,128)(2,1)}, bf16[512,768]{1,0:T(8,128)(2,1)S(1)}, u32[]{:S(2)}, u32[]{:S(2)}) %collective-permute-start.7) | collective-permute-done | bytes 786464 | tf_op jit(solution)/shard_map/ppermute | solution.py:22
  534.2 52.3 %conditional.100 = ((f32[768,3072]{1,0:T(8,128)}, f32[3072,768]{1,0:T(8,128)}, f32[7,768]{1,0:T(8,128)}, bf16[512,768]{1,0:T(8,128)(2,1)})) conditional(s32[]{:T(128)} %convert_element_type.1459, (f32[768,3072]{1,0:T(8,128)}, f32[3072,768]{1,0:T(8,128)}, f32[7,768]{1,0:T(8,128)}) %tuple.754, (s32[]{:T(128)}, f32[4,512,3072]{2,1,0:T(8,128)}, ...), branch_computations={%region_237.238_spmd, %region_238.277_spmd} | conditional | flops 9726219264 | bytes 193759808 | solution.py:323
  541.6 39.6 %conditional.44 = (f32[768,3072]{1,0:T(8,128)}, f32[3072,768]{1,0:T(8,128)}, f32[7,768]{1,0:T(8,128)}, bf16[512,768]{1,0:T(8,128)(2,1)}) conditional(s32[]{:T(128)} %clamp.51, (f32[512,768]{1,0:T(8,128)S(1)}, f32[7,768]{1,0:T(8,128)S(1)}, f32[512,3072]{1,0:T(8,128)}, f32[512,768]{1,0:T(8,128)S(1)}, ...), branch_computations={%region_239.249_spmd, %region_250.257_spmd, %region_258.268_spmd, ... | conditional | flops 9725826048 | bytes 178817344
  549.2 8.8 fusion.1031
  572.8 8.2 convolution_add_fusion.20
  589.8 10.9 collective-permute-done.8
  601.9 47.0 %conditional.101 = ((f32[768,3072]{1,0:T(8,128)}, f32[3072,768]{1,0:T(8,128)}, f32[7,768]{1,0:T(8,128)}, bf16[512,768]{1,0:T(8,128)(2,1)})) conditional(s32[]{:T(128)} %convert_element_type.1463, (f32[768,3072]{1,0:T(8,128)}, f32[3072,768]{1,0:T(8,128)}, f32[7,768]{1,0:T(8,128)}) %tuple.756, (s32[]{:T(128)}, f32[4,512,3072]{2,1,0:T(8,128)}, ...), branch_computations={%region_280.281_spmd, %region_281.320_spmd} | conditional | flops 9726219264 | bytes 193759808 | solution.py:323
  609.3 39.6 %conditional.45 = (f32[768,3072]{1,0:T(8,128)}, f32[3072,768]{1,0:T(8,128)}, f32[7,768]{1,0:T(8,128)}, bf16[512,768]{1,0:T(8,128)(2,1)}) conditional(s32[]{:T(128)} %clamp.52, (f32[512,768]{1,0:T(8,128)S(1)}, f32[7,768]{1,0:T(8,128)S(1)}, f32[512,3072]{1,0:T(8,128)}, f32[512,768]{1,0:T(8,128)S(1)}, ...), branch_computations={%region_282.292_spmd, %region_293.300_spmd, %region_301.311_spmd, ... | conditional | flops 9725826048 | bytes 178817344
  616.8 8.8 fusion.1162
  640.3 8.2 convolution_add_fusion.25
  648.9 30.8 %collective-permute-start.9 = (bf16[512,768]{1,0:T(8,128)(2,1)}, bf16[512,768]{1,0:T(8,128)(2,1)S(1)}, u32[]{:S(2)}, u32[]{:S(2)}) collective-permute-start(bf16[512,768]{1,0:T(8,128)(2,1)} %get-tuple-element.2884), channel_id=1, source_target_pairs={{8,0},{16,8},{24,16},{9,1},{17,9},{25,17},{10,2},{18,10},{26,18},{... | collective-permute-start | bytes 2359304 | tf_op jit(solution)/shard_map/ppermute | solution.py:22
  690.2 52.4 %conditional.102 = ((f32[768,3072]{1,0:T(8,128)}, f32[3072,768]{1,0:T(8,128)}, f32[7,768]{1,0:T(8,128)}, bf16[512,768]{1,0:T(8,128)(2,1)})) conditional(s32[]{:T(128)} %convert_element_type.1467, (f32[768,3072]{1,0:T(8,128)}, f32[3072,768]{1,0:T(8,128)}, f32[7,768]{1,0:T(8,128)}) %tuple.758, (s32[]{:T(128)}, f32[4,512,3072]{2,1,0:T(8,128)}, ...), branch_computations={%region_323.324_spmd, %region_324.363_spmd} | conditional | flops 9726219264 | bytes 193759808 | solution.py:323
  697.6 39.5 %conditional.46 = (f32[768,3072]{1,0:T(8,128)}, f32[3072,768]{1,0:T(8,128)}, f32[7,768]{1,0:T(8,128)}, bf16[512,768]{1,0:T(8,128)(2,1)}) conditional(s32[]{:T(128)} %clamp.53, (f32[512,768]{1,0:T(8,128)S(1)}, f32[7,768]{1,0:T(8,128)S(1)}, f32[512,3072]{1,0:T(8,128)}, f32[512,768]{1,0:T(8,128)S(1)}, ...), branch_computations={%region_325.335_spmd, %region_336.343_spmd, %region_344.354_spmd, ... | conditional | flops 9725826048 | bytes 178817344
  705.3 8.8 fusion.1293
  728.8 8.2 convolution_add_fusion.30
  742.6 32.2 %collective-permute-start.10 = (bf16[512,768]{1,0:T(8,128)(2,1)}, bf16[512,768]{1,0:T(8,128)(2,1)S(1)}, u32[]{:S(2)}, u32[]{:S(2)}) collective-permute-start(bf16[512,768]{1,0:T(8,128)(2,1)} %get-tuple-element.2888), channel_id=1, source_target_pairs={{8,0},{16,8},{24,16},{9,1},{17,9},{25,17},{10,2},{18,10},{26,18},{... | collective-permute-start | bytes 2359304 | tf_op jit(solution)/shard_map/ppermute | solution.py:22
  785.3 52.6 %conditional.103 = ((f32[768,3072]{1,0:T(8,128)}, f32[3072,768]{1,0:T(8,128)}, f32[7,768]{1,0:T(8,128)}, bf16[512,768]{1,0:T(8,128)(2,1)})) conditional(s32[]{:T(128)} %convert_element_type.1471, (f32[768,3072]{1,0:T(8,128)}, f32[3072,768]{1,0:T(8,128)}, f32[7,768]{1,0:T(8,128)}) %tuple.760, (s32[]{:T(128)}, f32[4,512,3072]{2,1,0:T(8,128)}, ...), branch_computations={%region_366.367_spmd, %region_367.406_spmd} | conditional | flops 9726219264 | bytes 193759808 | solution.py:323
  792.7 39.6 %conditional.47 = (f32[768,3072]{1,0:T(8,128)}, f32[3072,768]{1,0:T(8,128)}, f32[7,768]{1,0:T(8,128)}, bf16[512,768]{1,0:T(8,128)(2,1)}) conditional(s32[]{:T(128)} %clamp.54, (f32[512,768]{1,0:T(8,128)S(1)}, f32[7,768]{1,0:T(8,128)S(1)}, f32[512,3072]{1,0:T(8,128)}, f32[512,768]{1,0:T(8,128)S(1)}, ...), branch_computations={%region_368.378_spmd, %region_379.386_spmd, %region_387.397_spmd, ... | conditional | flops 9725826048 | bytes 178817344
  800.4 8.8 fusion.1424
  823.9 8.2 convolution_add_fusion.35
  838.0 32.1 %collective-permute-start.11 = (bf16[512,768]{1,0:T(8,128)(2,1)}, bf16[512,768]{1,0:T(8,128)(2,1)S(1)}, u32[]{:S(2)}, u32[]{:S(2)}) collective-permute-start(bf16[512,768]{1,0:T(8,128)(2,1)} %get-tuple-element.2892), channel_id=1, source_target_pairs={{8,0},{16,8},{24,16},{9,1},{17,9},{25,17},{10,2},{18,10},{26,18},{... | collective-permute-start | bytes 2359304 | tf_op jit(solution)/shard_map/ppermute | solution.py:22
  887.0 40.8 %psum.23 = f32[1,7,768]{2,0,1:T(1,128)} all-reduce(f32[1,7,768]{2,0,1:T(1,128)S(1)} %broadcast_in_dim.975), channel_id=1, replica_groups=mesh['section'=4,'dp'=8] {'dp'}, use_global_device_ids=true, to_apply=%region_452.453 | all-reduce | flops 5376 | bytes 43008 | tf_op jit(solution)/shard_map/psum | solution.py:351
  927.8 95.4 %reduce-scatter.9.cloned.1.call-done = bf16[1,512,768]{2,1,0:T(8,128)(2,1)} async-done(((bf16[4,512,768]{2,1,0:T(8,128)(2,1)}), bf16[1,512,768]{2,1,0:T(8,128)(2,1)}) %reduce-scatter.9.cloned.1.call-update) | async-done | bytes 786448
  1023.2 375.9 %all-reduce.19.cloned.1.call-done = (f32[1,768,3072]{2,1,0:T(8,128)}, f32[1,3072,768]{2,1,0:T(8,128)}) async-done(((f32[1,768,3072]{2,1,0:T(8,128)}, f32[1,3072,768]{2,1,0:T(8,128)}), (f32[1,768,3072]{2,1,0:T(8,128)}, f32[1,3072,768]{2,1,0:T(8,128)})) %all-reduce.19.cloned.1.call-update) | async-done | bytes 18874384 | tf_op jit(solution)/shard_map/psum | solution.py:351
  1399.1 8.8 copy.2578
  (485 shorter events, 371.9 us)
Async XLA Ops:
  7.2 47.9 %all-gather.3.cloned.1.call-start = ((), (), s32[]{:S(2)}) async-start(), calls=%async_computation.2 | async-start | bytes 3932160 | tf_op jit(solution)/shard_map/all_gather | solution.py:173
  7.9 416.8 %all-gather.5.cloned.1.call-start = ((), (), s32[]{:S(2)}) async-start(), calls=%async_computation.3 | async-start | bytes 3932160 | tf_op jit(solution)/shard_map/all_gather | solution.py:174
  8.6 919.2 %reduce-scatter.7.cloned.1.call-start = ((), (), s32[]{:S(2)}) async-start(), calls=%async_computation.4 | async-start | bytes 3932160
  16.3 40.4 %copy-start.126 = (s32[4,1]{0,1:T(1,128)}, s32[4,1]{0,1:T(1,128)S(1)}, u32[]{:S(2)}) copy-start(s32[4,1]{0,1:T(1,128)S(1)} %reduce-window.110) | copy-start | bytes 52
  16.5 40.2 %copy-start.128 = (s32[4,1]{0,1:T(1,128)}, s32[4,1]{0,1:T(1,128)S(1)}, u32[]{:S(2)}) copy-start(s32[4,1]{0,1:T(1,128)S(1)} %reduce-window.111) | copy-start | bytes 52
  16.6 40.1 %copy-start.130 = (s32[4]{0:T(128)}, s32[4]{0:T(128)S(1)}, u32[]{:S(2)}) copy-start(s32[4]{0:T(128)S(1)} %convert_reduce_fusion.7) | copy-start | bytes 52
  16.8 40.0 %copy-start.132 = (s32[4]{0:T(128)}, s32[4]{0:T(128)S(1)}, u32[]{:S(2)}) copy-start(s32[4]{0:T(128)S(1)} %convert_reduce_fusion.8) | copy-start | bytes 52
  22.3 34.4 %copy-start.107 = (s32[4]{0:T(128)}, s32[4]{0:T(128)S(1)}, u32[]{:S(2)}) copy-start(s32[4]{0:T(128)S(1)} %convert_reduce_fusion.2) | copy-start | bytes 52
  22.4 34.3 %copy-start.109 = (s32[4]{0:T(128)}, s32[4]{0:T(128)S(1)}, u32[]{:S(2)}) copy-start(s32[4]{0:T(128)S(1)} %convert_reduce_fusion.3) | copy-start | bytes 52
  66.7 53.9 %collective-permute-start = (bf16[512,768]{1,0:T(8,128)(2,1)}, bf16[512,768]{1,0:T(8,128)(2,1)S(1)}, u32[]{:S(2)}, u32[]{:S(2)}) collective-permute-start(bf16[512,768]{1,0:T(8,128)(2,1)} %get-tuple-element.2858), channel_id=1, source_target_pairs={{0,8},{8,16},{16,24},{1,9},{9,17},{17,25},{2,10},{10,18},{18,26},{... | collective-permute-start | bytes 2359304 | tf_op jit(solution)/shard_map/ppermute | solution.py:22
  144.9 43.7 %collective-permute-start.1 = (bf16[512,768]{1,0:T(8,128)(2,1)}, bf16[512,768]{1,0:T(8,128)(2,1)S(1)}, u32[]{:S(2)}, u32[]{:S(2)}) collective-permute-start(bf16[512,768]{1,0:T(8,128)(2,1)} %get-tuple-element.2859), channel_id=1, source_target_pairs={{0,8},{8,16},{16,24},{1,9},{9,17},{17,25},{2,10},{10,18},{18,26},{... | collective-permute-start | bytes 2359304 | tf_op jit(solution)/shard_map/ppermute | solution.py:22
  146.9 10.2 copy-start.17
  146.9 10.2 copy-start.58
  146.9 10.2 copy-start.74
  168.7 20.1 %copy-start.139 = (s32[4]{0:T(128)S(1)}, s32[4]{0:T(128)}, u32[]{:S(2)}) copy-start(s32[4]{0:T(128)} %copy-done.138) | copy-start | bytes 52
  218.1 40.1 %collective-permute-start.2 = (bf16[512,768]{1,0:T(8,128)(2,1)}, bf16[512,768]{1,0:T(8,128)(2,1)S(1)}, u32[]{:S(2)}, u32[]{:S(2)}) collective-permute-start(bf16[512,768]{1,0:T(8,128)(2,1)} %get-tuple-element.2860), channel_id=1, source_target_pairs={{0,8},{8,16},{16,24},{1,9},{9,17},{17,25},{2,10},{10,18},{18,26},{... | collective-permute-start | bytes 2359304 | tf_op jit(solution)/shard_map/ppermute | solution.py:22
  241.7 16.6 %copy-start.106 = (f32[4,4]{1,0:T(4,128)S(1)}, f32[4,4]{1,0:T(4,128)}, u32[]{:S(2)}) copy-start(f32[4,4]{1,0:T(4,128)} %fusion.1657) | copy-start | bytes 196
  241.7 16.6 %copy-start.137 = (s32[4]{0:T(128)S(1)}, s32[4]{0:T(128)}, u32[]{:S(2)}) copy-start(s32[4]{0:T(128)} %copy-done.136) | copy-start | bytes 52
  274.8 45.9 %collective-permute-start.3 = (bf16[512,768]{1,0:T(8,128)(2,1)}, bf16[512,768]{1,0:T(8,128)(2,1)S(1)}, u32[]{:S(2)}, u32[]{:S(2)}) collective-permute-start(bf16[512,768]{1,0:T(8,128)(2,1)} %get-tuple-element.2861), channel_id=1, source_target_pairs={{0,8},{8,16},{16,24},{1,9},{9,17},{17,25},{2,10},{10,18},{18,26},{... | collective-permute-start | bytes 2359304 | tf_op jit(solution)/shard_map/ppermute | solution.py:22
  276.8 10.3 copy-start.19
  276.8 10.2 copy-start.60
  276.8 10.2 copy-start.70
  298.6 22.2 %copy-start.105 = (f32[4,4]{1,0:T(4,128)S(1)}, f32[4,4]{1,0:T(4,128)}, u32[]{:S(2)}) copy-start(f32[4,4]{1,0:T(4,128)} %fusion.1658) | copy-start | bytes 196
  298.6 22.2 %copy-start.135 = (s32[4]{0:T(128)S(1)}, s32[4]{0:T(128)}, u32[]{:S(2)}) copy-start(s32[4]{0:T(128)} %copy-done.134) | copy-start | bytes 52
  344.6 23.7 %collective-permute-start.4 = (bf16[512,768]{1,0:T(8,128)(2,1)}, bf16[512,768]{1,0:T(8,128)(2,1)S(1)}, u32[]{:S(2)}, u32[]{:S(2)}) collective-permute-start(bf16[512,768]{1,0:T(8,128)(2,1)} %get-tuple-element.2862), channel_id=1, source_target_pairs={{0,8},{8,16},{16,24},{1,9},{9,17},{17,25},{2,10},{10,18},{18,26},{... | collective-permute-start | bytes 2359304 | tf_op jit(solution)/shard_map/ppermute | solution.py:22
  346.6 10.2 copy-start.20
  346.6 10.2 copy-start.61
  346.6 10.2 copy-start.72
  382.6 20.0 %collective-permute-start.5 = (bf16[512,768]{1,0:T(8,128)(2,1)}, bf16[512,768]{1,0:T(8,128)(2,1)S(1)}, u32[]{:S(2)}, u32[]{:S(2)}) collective-permute-start(bf16[512,768]{1,0:T(8,128)(2,1)} %get-tuple-element.2863), channel_id=1, source_target_pairs={{0,8},{8,16},{16,24},{1,9},{9,17},{17,25},{2,10},{10,18},{18,26},{... | collective-permute-start | bytes 2359304 | tf_op jit(solution)/shard_map/ppermute | solution.py:22
  442.4 20.0 %collective-permute-start.6 = (bf16[512,768]{1,0:T(8,128)(2,1)}, bf16[512,768]{1,0:T(8,128)(2,1)S(1)}, u32[]{:S(2)}, u32[]{:S(2)}) collective-permute-start(bf16[512,768]{1,0:T(8,128)(2,1)} %get-tuple-element.2872), channel_id=1, source_target_pairs={{8,0},{16,8},{24,16},{9,1},{17,9},{25,17},{10,2},{18,10},{26,18},{... | collective-permute-start | bytes 2359304 | tf_op jit(solution)/shard_map/ppermute | solution.py:22
  448.8 14.8 %copy-start.116 = (s32[4]{0:T(128)S(1)}, s32[4]{0:T(128)}, u32[]{:S(2)}) copy-start(s32[4]{0:T(128)} %copy-done.115) | copy-start | bytes 52
  448.8 14.8 %copy-start.99 = (f32[4,4]{1,0:T(4,128)S(1)}, f32[4,4]{1,0:T(4,128)}, u32[]{:S(2)}) copy-start(f32[4,4]{1,0:T(4,128)} %fusion.1662) | copy-start | bytes 196
  448.8 574.4 %reduce-scatter.9.cloned.1.call-start = ((), (), s32[]{:S(2)}) async-start(), calls=%async_computation.5 | async-start | bytes 3932160
  449.0 22.7 %copy-start.113 = (s32[4]{0:T(128)}, s32[4]{0:T(128)S(1)}, u32[]{:S(2)}) copy-start(s32[4]{0:T(128)S(1)} %convert_reduce_fusion) | copy-start | bytes 52
  449.2 22.6 %copy-start.117 = (s32[4]{0:T(128)}, s32[4]{0:T(128)S(1)}, u32[]{:S(2)}) copy-start(s32[4]{0:T(128)S(1)} %convert_reduce_fusion.1) | copy-start | bytes 52
  469.8 64.3 %copy-start.112 = (s32[4]{0:T(128)S(1)}, s32[4]{0:T(128)}, u32[]{:S(2)}) copy-start(s32[4]{0:T(128)} %copy-done.111) | copy-start | bytes 52
  469.8 63.1 %collective-permute-start.7 = (bf16[512,768]{1,0:T(8,128)(2,1)}, bf16[512,768]{1,0:T(8,128)(2,1)S(1)}, u32[]{:S(2)}, u32[]{:S(2)}) collective-permute-start(bf16[512,768]{1,0:T(8,128)(2,1)} %get-tuple-element.2876), channel_id=1, source_target_pairs={{8,0},{16,8},{24,16},{9,1},{17,9},{25,17},{10,2},{18,10},{26,18},{... | collective-permute-start | bytes 2359304 | tf_op jit(solution)/shard_map/ppermute | solution.py:22
  534.2 54.2 %copy-start.123 = (s32[4]{0:T(128)S(1)}, s32[4]{0:T(128)}, u32[]{:S(2)}) copy-start(s32[4]{0:T(128)} %iota_subtract_fusion.2) | copy-start | bytes 52
  561.8 11.0 slice-start.30
  586.4 15.4 %copy-start.110 = (s32[4]{0:T(128)S(1)}, s32[4]{0:T(128)}, u32[]{:S(2)}) copy-start(s32[4]{0:T(128)} %copy-done.109) | copy-start | bytes 52
  586.4 14.2 %collective-permute-start.8 = (bf16[512,768]{1,0:T(8,128)(2,1)}, bf16[512,768]{1,0:T(8,128)(2,1)S(1)}, u32[]{:S(2)}, u32[]{:S(2)}) collective-permute-start(bf16[512,768]{1,0:T(8,128)(2,1)} %get-tuple-element.2880), channel_id=1, source_target_pairs={{8,0},{16,8},{24,16},{9,1},{17,9},{25,17},{10,2},{18,10},{26,18},{... | collective-permute-start | bytes 2359304 | tf_op jit(solution)/shard_map/ppermute | solution.py:22
  629.3 11.0 slice-start.32
  648.9 40.0 %collective-permute-start.9 = (bf16[512,768]{1,0:T(8,128)(2,1)}, bf16[512,768]{1,0:T(8,128)(2,1)S(1)}, u32[]{:S(2)}, u32[]{:S(2)}) collective-permute-start(bf16[512,768]{1,0:T(8,128)(2,1)} %get-tuple-element.2884), channel_id=1, source_target_pairs={{8,0},{16,8},{24,16},{9,1},{17,9},{25,17},{10,2},{18,10},{26,18},{... | collective-permute-start | bytes 2359304 | tf_op jit(solution)/shard_map/ppermute | solution.py:22
  717.8 11.0 slice-start.34
  742.6 41.5 %collective-permute-start.10 = (bf16[512,768]{1,0:T(8,128)(2,1)}, bf16[512,768]{1,0:T(8,128)(2,1)S(1)}, u32[]{:S(2)}, u32[]{:S(2)}) collective-permute-start(bf16[512,768]{1,0:T(8,128)(2,1)} %get-tuple-element.2888), channel_id=1, source_target_pairs={{8,0},{16,8},{24,16},{9,1},{17,9},{25,17},{10,2},{18,10},{26,18},{... | collective-permute-start | bytes 2359304 | tf_op jit(solution)/shard_map/ppermute | solution.py:22
  813.0 11.0 slice-start.36
  838.0 41.4 %collective-permute-start.11 = (bf16[512,768]{1,0:T(8,128)(2,1)}, bf16[512,768]{1,0:T(8,128)(2,1)S(1)}, u32[]{:S(2)}, u32[]{:S(2)}) collective-permute-start(bf16[512,768]{1,0:T(8,128)(2,1)} %get-tuple-element.2892), channel_id=1, source_target_pairs={{8,0},{16,8},{24,16},{9,1},{17,9},{25,17},{10,2},{18,10},{26,18},{... | collective-permute-start | bytes 2359304 | tf_op jit(solution)/shard_map/ppermute | solution.py:22
  885.7 513.4 %all-reduce.19.cloned.1.call-start = ((), (), s32[]{:S(2)}) async-start(), calls=%async_computation.6 | async-start | bytes 37748736 | tf_op jit(solution)/shard_map/psum | solution.py:351
  (63 other events, 386.0 us)
Sparse Core Ops, SparseCore 0:
  9.8 45.1 all-gather.2
  56.9 50.8 all-gather.4
  448.9 75.8 reduce-scatter.6
  885.8 137.3 reduce-scatter.8
  1026.2 372.8 all-reduce.18
where the time goes:
time: 1430 us; the launch traced here: 1420 us
  waiting for transfers between devices  688 us (48%)
  matrix products  171 us (12%)
  local copies, waits for them, and re-layouts  154 us (11%)
  other arithmetic  128 us (9%)
  starting transfers between devices  114 us (8%)
  loops' own time  108 us (8%)
  blocking collectives  40.8 us (3%)
  between operations  15.2 us (1%)
    psum x1, waiting for transfers between devices, local(): lax.psum((sum_wide, sum_down, sum_vector), 'dp')  376 us
    ppermute x12, waiting for transfers between devices, shifted(): return lax.ppermute(shard, axis, pairs)  183 us
    dot_general x24, matrix products, product(): return jnp.dot(left_side, right_side, preferred_element_type=jnp.float32)  171 us
    ppermute x12, starting transfers between devices, shifted(): return lax.ppermute(shard, axis, pairs)  114 us
    unnamed x7, waiting for transfers between devices  97.3 us
    dynamic_update_slice x28, other arithmetic, put_slot(): lax.dynamic_update_index_in_dim(buffer, jnp.where(running, item, previous...  81.5 us
    dynamic_slice x24, local copies, waits for them, and re-layouts, put_slot(): previous = lax.dynamic_index_in_dim(buffer, batch_slot, 0, keepdims=False)  68.3 us
    unnamed x8, loops' own time  44.6 us
  transfers between devices with their start and end apart: 17, of which 14 were waited for; matrix products, arithmetic and copies ran while one was open for 30% of the time, Pallas kernels for 0%

commit v1 on v0

v1 whole, which is shorter than its diff:
```python
from functools import partial

import jax
import jax.numpy as jnp
from jax import lax
from jax.experimental import pallas as pl
from jax.experimental.pallas import tpu as pltpu
from jax.sharding import PartitionSpec as P

HEADS = 12
SEG = 128
SEGS = 4
EPSILON = 1e-05
SCORE_SCALE = 0.125
MASKED = -1e30
AXES = ("section", "dp")
BF = jnp.bfloat16
F32 = jnp.float32

NN = (((1,), (0,)), ((), ()))
NT = (((1,), (1,)), ((), ()))
TN = (((0,), (0,)), ((), ()))

GELU_A = 0.7978845608028654
GELU_B = 0.044715

ATT_RINGS = ((0, 1, 3, 2), (0, 2, 3, 1))
MLP_RINGS = ((1, 3, 2, 0), (1, 0, 2, 3))


def mm(left, right, dims=NN):
    return lax.dot_general(left, right, dims, preferred_element_type=F32)


def permute(shard, move, keep=lambda s, r: True):
    sections, replicas = lax.axis_size("section"), lax.axis_size("dp")
    pairs = []
    for s in range(sections):
        for r in range(replicas):
            if keep(s, r):
                t, q = move(s, r)
                pairs.append((s * replicas + r, t * replicas + q))
    return lax.ppermute(shard, AXES, pairs)


def swap_core(shard):
    return permute(shard, lambda s, r: (s, r ^ 1))


def swap_section(shard, bits):
    return permute(shard, lambda s, r: (s ^ bits, r))


def swap_dp(shard, bits):
    return permute(shard, lambda s, r: (s, r ^ bits))


def broadcast(parts, rings, position):
    result = []
    for part in parts:
        hops = [part]
        for stage in range(3):
            hops.append(
                permute(
                    hops[-1],
                    lambda s, r: (rings[r & 1][stage + 1], r),
                    lambda s, r: rings[r & 1][stage] == s,
                )
            )
        value = hops[3]
        for stage in (2, 1, 0):
            value = jnp.where(position == stage, hops[stage], value)
        result.append(value)
    return result


def ring_position(rings, section, core):
    position = jnp.int32(0)
    for c in range(2):
        for k, s in enumerate(rings[c]):
            position = jnp.where((section == s) & (core == c), k, position)
    return position


def pick(stack, index):
    return lax.dynamic_index_in_dim(stack, index, 0, keepdims=False)


def reduce_pieces(grad, section, owner):
    replicas = lax.axis_size("dp")
    total = pick(grad, section).astype(F32)
    others = [swap_section(pick(grad, section ^ bits), bits) for bits in (1, 2, 3)]
    for other in others:
        total = total + other.astype(F32)
    total = total.astype(BF)
    bits = 2
    while bits < replicas:
        total = (total.astype(F32) + swap_dp(total, bits).astype(F32)).astype(BF)
        bits *= 2
    arrived = [
        permute(total, lambda s, r: (owner, r), lambda s, r: s == owner ^ bits) for bits in (1, 2, 3)
    ]
    quarters = [None] * 4
    quarters[owner] = total
    for bits, value in zip((1, 2, 3), arrived):
        quarters[owner ^ bits] = value
    return jnp.stack(quarters)


def norm_parts(values):
    center = values - jnp.mean(values, -1, keepdims=True)
    spread = jnp.mean(center * center, -1, keepdims=True)
    scale = lax.rsqrt(spread + EPSILON)
    return center * scale, scale


def norm_rows(values, vec_ref):
    hat, _ = norm_parts(values)
    return hat * vec_ref[0:1, :] + vec_ref[1:2, :]


def norm_back(values, grad_normed, vec_ref):
    hat, scale = norm_parts(values)
    inner = grad_normed * vec_ref[0:1, :]
    first = jnp.mean(inner, -1, keepdims=True)
    second = jnp.mean(inner * hat, -1, keepdims=True)
    return scale * (inner - first - hat * second), grad_normed * hat


def column_sum(values):
    return jnp.sum(values, 0, keepdims=True)


def gelu_parts(hidden):
    square = hidden * hidden
    inner = GELU_A * hidden * (1.0 + GELU_B * square)
    t = jnp.tanh(inner)
    half = 0.5 * (1.0 + t)
    slope = half + 0.5 * hidden * (1.0 - t * t) * (GELU_A * (1.0 + 3.0 * GELU_B * square))
    return hidden * half, slope


def two_heads(pair):
    low = lax.broadcasted_iota(jnp.int32, pair.shape, 1) < 64
    zero = jnp.zeros_like(pair)
    return jnp.concatenate([jnp.where(low, pair, zero), jnp.where(low, zero, pair)], 0)


def join_heads(both):
    rows = both.shape[0] // 2
    low = lax.broadcasted_iota(jnp.int32, (rows, both.shape[1]), 1) < 64
    return jnp.where(low, both[:rows], both[rows:])


def softmax_rows(scores):
    powers = jnp.exp(scores - jnp.max(scores, -1, keepdims=True))
    return powers / jnp.sum(powers, -1, keepdims=True)


def att_fwd_kernel(own_ref, sib_ref, wq, wk, wv, wo, vec_ref, q_ref, k_ref, v_ref, a_ref, p_ref, u_ref):
    rows = own_ref.shape[0]
    for pack, ref in enumerate((own_ref, sib_ref)):

        @pl.loop(0, rows // SEG)
        def _(i):
            at = pl.multiple_of(i * SEG, SEG)
            u_ref[pl.ds(pack * rows + at, SEG), :] = norm_rows(ref[pl.ds(at, SEG), :].astype(F32), vec_ref).astype(BF)

    for pack in range(2):
        span = slice(pack * rows, (pack + 1) * rows)
        u = u_ref[span, :]
        q_ref[span, :] = mm(u, wq[...]).astype(BF)
        k_ref[span, :] = mm(u, wk[...]).astype(BF)
        v_ref[span, :] = mm(u, wv[...]).astype(BF)

    @pl.loop(0, 2 * rows // SEG)
    def _(i):
        at = pl.ds(pl.multiple_of(i * SEG, SEG), SEG)
        for pair in range(q_ref.shape[1] // 128):
            lanes = slice(pair * 128, (pair + 1) * 128)
            scores = mm(two_heads(q_ref[at, lanes]), k_ref[at, lanes], NT) * SCORE_SCALE
            weights = softmax_rows(scores).astype(BF)
            a_ref[at, lanes] = join_heads(mm(weights, v_ref[at, lanes])).astype(BF)

    for pack in range(2):
        span = slice(pack * rows, (pack + 1) * rows)
        p_ref[span, :] = mm(a_ref[span, :], wo[...]).astype(BF)


def att_bwd_kernel(
    own_ref, sib_ref, gown_ref, gsib_ref, q_ref, k_ref, v_ref, a_ref, wq, wk, wv, wo, vec_ref,
    grad_ref, duown_ref, dusib_ref, u_ref, da_ref, dq_ref, dk_ref, dv_ref,
):
    rows = own_ref.shape[0]
    half = q_ref.shape[1]
    for pack, ref in enumerate((own_ref, sib_ref)):

        @pl.loop(0, rows // SEG)
        def _(i):
            at = pl.multiple_of(i * SEG, SEG)
            u_ref[pl.ds(pack * rows + at, SEG), :] = norm_rows(ref[pl.ds(at, SEG), :].astype(F32), vec_ref).astype(BF)

    for pack, ref in enumerate((gown_ref, gsib_ref)):
        da_ref[pack * rows : (pack + 1) * rows, :] = mm(ref[...], wo[...], NT).astype(BF)
    dwo = mm(a_ref[:rows, :], gown_ref[...], TN) + mm(a_ref[rows:, :], gsib_ref[...], TN)
    part = half // 4
    for quarter in range(4):
        grad_ref[quarter, 3 * part :, :] = dwo[quarter * part : (quarter + 1) * part, :].astype(BF)

    @pl.loop(0, 2 * rows // SEG)
    def _(i):
        at = pl.ds(pl.multiple_of(i * SEG, SEG), SEG)
        for pair in range(half // 128):
            lanes = slice(pair * 128, (pair + 1) * 128)
            q2 = two_heads(q_ref[at, lanes])
            da2 = two_heads(da_ref[at, lanes])
            k = k_ref[at, lanes]
            v = v_ref[at, lanes]
            probs = softmax_rows(mm(q2, k, NT) * SCORE_SCALE)
            dy = mm(da2, v, NT)
            ds = (probs * (dy - jnp.sum(dy * probs, -1, keepdims=True))).astype(BF)
            dv_ref[at, lanes] = mm(probs.astype(BF), da2, TN).astype(BF)
            dq_ref[at, lanes] = (join_heads(mm(ds, k)) * SCORE_SCALE).astype(BF)
            dk_ref[at, lanes] = (mm(ds, q2, TN) * SCORE_SCALE).astype(BF)

    for pack, out in enumerate((duown_ref, dusib_ref)):
        span = slice(pack * rows, (pack + 1) * rows)
        du = mm(dq_ref[span, :], wq[...], NT) + mm(dk_ref[span, :], wk[...], NT) + mm(dv_ref[span, :], wv[...], NT)
        out[...] = du.astype(out.dtype)
    dwq = mm(u_ref[...], dq_ref[...], TN)
    for quarter in range(4):
        grad_ref[quarter, : 2 * part, :half] = dwq[quarter * 2 * part : (quarter + 1) * 2 * part, :].astype(BF)
    dwk = mm(u_ref[...], dk_ref[...], TN)
    for quarter in range(4):
        grad_ref[quarter, : 2 * part, half:] = dwk[quarter * 2 * part : (quarter + 1) * 2 * part, :].astype(BF)
    dwv = mm(u_ref[...], dv_ref[...], TN)
    for quarter in range(4):
        grad_ref[quarter, 2 * part : 3 * part, :half] = dwv[quarter * part : (quarter + 1) * part, :].astype(BF)
        grad_ref[quarter, 2 * part : 3 * part, half:] = dwv[half + quarter * part : half + (quarter + 1) * part, :].astype(BF)


def att_done_kernel(x_ref, g_ref, duown_ref, dusib_ref, vec_ref, out_ref, small_ref):
    small_ref[...] = jnp.zeros_like(small_ref)

    @pl.loop(0, x_ref.shape[0] // SEG)
    def _(i):
        at = pl.ds(pl.multiple_of(i * SEG, SEG), SEG)
        du = duown_ref[at, :] + dusib_ref[at, :].astype(F32)
        grad = g_ref[at, :].astype(F32)
        back, gain = norm_back(x_ref[at, :].astype(F32), du, vec_ref)
        out_ref[at, :] = (grad + back).astype(BF)
        small_ref[0:1, :] += column_sum(gain)
        small_ref[1:2, :] += column_sum(du)
        small_ref[2:3, :] += column_sum(grad)


def att_join_kernel(own_ref, sib_ref, p_ref, r_ref, avec_ref, mvec_ref, h_ref, u_ref):
    rows = own_ref.shape[0]
    for pack, ref in enumerate((own_ref, sib_ref)):

        @pl.loop(0, rows // SEG)
        def _(i):
            at = pl.multiple_of(i * SEG, SEG)
            here, there = pl.ds(pack * rows + at, SEG), pl.ds((1 - pack) * rows + at, SEG)
            branch = p_ref[here, :].astype(F32) + r_ref[there, :].astype(F32)
            out = (ref[pl.ds(at, SEG), :].astype(F32) + branch + avec_ref[2:3, :]).astype(BF)
            h_ref[here, :] = out
            u_ref[here, :] = norm_rows(out.astype(F32), mvec_ref).astype(BF)


def mlp_kernel(first, tile, u_ref, b_ref, w_ref, v_ref, *refs):
    if first:
        out_ref, du_ref, grad_ref = refs
        out_ref[...] = jnp.zeros_like(out_ref)
        du_ref[...] = jnp.zeros_like(du_ref)
    else:
        outin_ref, duin_ref, out_ref, du_ref, grad_ref = refs
        out_ref[...] = outin_ref[...]
        du_ref[...] = duin_ref[...]
    u = u_ref[...]
    b = b_ref[...]
    features, hidden = w_ref.shape
    quarter_w, quarter_v = features // 4, hidden // 4
    for j in range(hidden // tile):
        at = slice(j * tile, (j + 1) * tile)
        w, v = w_ref[:, at], v_ref[at, :]
        active, slope = gelu_parts(mm(u, w))
        active = active.astype(BF)
        out_ref[...] += mm(active, v)
        dh = (mm(b, v, NT) * slope).astype(BF)
        du_ref[...] += mm(dh, w, NT)
        dw = mm(u, dh, TN)
        for quarter in range(4):
            grad_ref[quarter, :quarter_w, at] = dw[quarter * quarter_w : (quarter + 1) * quarter_w, :].astype(BF)
        dv = mm(active, b, TN).astype(BF)
        done = 0
        while done < tile:
            row = j * tile + done
            quarter, inside = row // quarter_v, row % quarter_v
            count = min(quarter_v - inside, tile - done)
            grad_ref[quarter, quarter_w + inside : quarter_w + inside + count, :] = dv[done : done + count, :]
            done += count


def mlp_done_kernel(h_ref, b_ref, out_ref, outr_ref, du_ref, dur_ref, vec_ref, next_ref, grad_ref, small_ref):
    small_ref[...] = jnp.zeros_like(small_ref)

    @pl.loop(0, h_ref.shape[0] // SEG)
    def _(i):
        at = pl.ds(pl.multiple_of(i * SEG, SEG), SEG)
        values = h_ref[at, :].astype(F32)
        branch = out_ref[at, :] + outr_ref[at, :].astype(F32)
        next_ref[at, :] = (values + branch + vec_ref[2:3, :]).astype(BF)
        du = du_ref[at, :] + dur_ref[at, :].astype(F32)
        grad = b_ref[at, :].astype(F32)
        back, gain = norm_back(values, du, vec_ref)
        grad_ref[at, :] = (grad + back).astype(BF)
        small_ref[0:1, :] += column_sum(gain)
        small_ref[1:2, :] += column_sum(du)
        small_ref[2:3, :] += column_sum(grad)


def cls_mlp_kernel(weights_too, h_ref, b_ref, w_ref, v_ref, vec_ref, *refs):
    if weights_too:
        mainw_ref, mainv_ref, small_ref, dw_ref, dv_ref, u_ref, out_acc, du_acc = refs
    else:
        out_ref, grad_ref, u_ref, out_acc, du_acc = refs
    j = pl.program_id(0)

    @pl.when(j == 0)
    def _():
        u_ref[...] = norm_rows(h_ref[...].astype(F32), vec_ref).astype(BF)
        out_acc[...] = jnp.zeros_like(out_acc)
        du_acc[...] = jnp.zeros_like(du_acc)

    u = u_ref[...]
    b = b_ref[...]
    active, slope = gelu_parts(mm(u, w_ref[...]))
    active = active.astype(BF)
    dh = (mm(b, v_ref[...], NT) * slope).astype(BF)
    du_acc[...] += mm(dh, w_ref[...], NT)
    if weights_too:
        dw_ref[...] = mainw_ref[...].astype(F32) + mm(u, dh, TN)
        dv_ref[...] = mainv_ref[...].astype(F32) + mm(active, b, TN)
    else:
        out_acc[...] += mm(active, v_ref[...])

    @pl.when(j == pl.num_programs(0) - 1)
    def _():
        values = h_ref[...].astype(F32)
        grad = b.astype(F32)
        back, gain = norm_back(values, du_acc[...], vec_ref)
        if weights_too:
            small_ref[...] = jnp.zeros_like(small_ref)
            small_ref[0:1, :] = column_sum(gain)
            small_ref[1:2, :] = column_sum(du_acc[...])
            small_ref[2:3, :] = column_sum(grad)
        else:
            out_ref[...] = (values + out_acc[...] + vec_ref[2:3, :]).astype(BF)
            grad_ref[...] = (grad + back).astype(BF)


def lifted_rows(h_ref, pos_ref, vec_ref):
    values = h_ref[...].astype(F32)
    pos = pos_ref[...]
    for p in range(SEGS):
        values = values + jnp.where(pos == p, vec_ref[3 + p : 4 + p, :], 0.0)
    return values


def cls_att_forward(values, col_ref, row_ref, w_ref, vec_ref):
    features = values.shape[1]
    u = norm_rows(values, vec_ref).astype(BF)
    triple = mm(u, w_ref[:, : 3 * features]).astype(BF)
    column = jnp.concatenate([col_ref[...], col_ref[...]], 0)
    mask = column == row_ref[...]
    probs, mixed = [], []
    for pair in range(features // 128):
        lanes = slice(pair * 128, (pair + 1) * 128)
        q2 = two_heads(triple[:, lanes])
        k = triple[:, features + pair * 128 : features + (pair + 1) * 128]
        v = triple[:, 2 * features + pair * 128 : 2 * features + (pair + 1) * 128]
        scores = jnp.where(mask, mm(q2, k, NT) * SCORE_SCALE, MASKED)
        probs.append(softmax_rows(scores))
        mixed.append(join_heads(mm(probs[-1].astype(BF), v)).astype(BF))
    return u, triple, probs, jnp.concatenate(mixed, 1)


def cls_att_fwd_kernel(h_ref, pos_ref, col_ref, row_ref, w_ref, vec_ref, out_ref):
    values = lifted_rows(h_ref, pos_ref, vec_ref)
    features = values.shape[1]
    _, _, _, mixed = cls_att_forward(values, col_ref, row_ref, w_ref, vec_ref)
    out_ref[...] = (values + mm(mixed, w_ref[:, 3 * features :]) + vec_ref[2:3, :]).astype(BF)


def cls_att_bwd_kernel(weights_too, h_ref, g_ref, pos_ref, col_ref, row_ref, w_ref, vec_ref, *refs):
    values = lifted_rows(h_ref, pos_ref, vec_ref)
    features = values.shape[1]
    u, triple, probs, mixed = cls_att_forward(values, col_ref, row_ref, w_ref, vec_ref)
    b = g_ref[...]
    da = mm(b, w_ref[:, 3 * features :], NT).astype(BF)
    dqs, dks, dvs = [], [], []
    for pair in range(features // 128):
        lanes = slice(pair * 128, (pair + 1) * 128)
        q2 = two_heads(triple[:, lanes])
        k = triple[:, features + pair * 128 : features + (pair + 1) * 128]
        v = triple[:, 2 * features + pair * 128 : 2 * features + (pair + 1) * 128]
        da2 = two_heads(da[:, lanes])
        y = probs[pair]
        dy = mm(da2, v, NT)
        ds = (y * (dy - jnp.sum(dy * y, -1, keepdims=True))).astype(BF)
        dvs.append(mm(y.astype(BF), da2, TN).astype(BF))
        dqs.append((join_heads(mm(ds, k)) * SCORE_SCALE).astype(BF))
        dks.append((mm(ds, q2, TN) * SCORE_SCALE).astype(BF))
    dtriple = jnp.concatenate(dqs + dks + dvs, 1)
    du = mm(dtriple, w_ref[:, : 3 * features], NT)
    back, gain = norm_back(values, du, vec_ref)
    grad = b.astype(F32)
    total = grad + back
    if weights_too:
        small_ref, dw_ref = refs

        @pl.when(pl.program_id(0) == 0)
        def _():
            small_ref[...] = jnp.zeros_like(small_ref)
            dw_ref[...] = jnp.zeros_like(dw_ref)

        small_ref[0:1, :] += column_sum(gain)
        small_ref[1:2, :] += column_sum(du)
        small_ref[2:3, :] += column_sum(grad)
        pos = pos_ref[...]
        for p in range(SEGS):
            small_ref[3 + p : 4 + p, :] += column_sum(jnp.where(pos == p, total, 0.0))
        for part in range(3):
            span = slice(part * features, (part + 1) * features)
            dw_ref[:, span] += mm(u, dtriple[:, span], TN)
        dw_ref[:, 3 * features :] += mm(mixed, b, TN)
    else:
        (out_ref,) = refs
        out_ref[...] = total.astype(BF)


def att_place_kernel(first_ref, second_ref, out_ref):
    half = first_ref.shape[2] // 2
    part = half // 4
    for core, ref in enumerate((first_ref, second_ref)):
        for quarter in range(4):
            rows = slice(quarter * 2 * part, (quarter + 1) * 2 * part)
            for kind in range(2):
                out_ref[rows, kind * 2 * half + core * half : kind * 2 * half + (core + 1) * half] = ref[
                    quarter, : 2 * part, kind * half : (kind + 1) * half
                ].astype(F32)
            for side in range(2):
                out_ref[
                    side * half + quarter * part : side * half + (quarter + 1) * part,
                    4 * half + core * half : 4 * half + (core + 1) * half,
                ] = ref[quarter, 2 * part : 3 * part, side * half : (side + 1) * half].astype(F32)
            out_ref[core * half + quarter * part : core * half + (quarter + 1) * part, 6 * half :] = ref[
                quarter, 3 * part :, :
            ].astype(F32)


VMEM = pl.BlockSpec(memory_space=pltpu.VMEM)
LIMIT = 50 * 2**20


def call(kernel, out_shapes, args, scratch=(), flops=0, moved=0, alias=None):
    return pl.pallas_call(
        kernel,
        out_shape=[jax.ShapeDtypeStruct(*shape) for shape in out_shapes],
        in_specs=[VMEM] * len(args),
        out_specs=[VMEM] * len(out_shapes),
        scratch_shapes=list(scratch),
        compiler_params=pltpu.CompilerParams(vmem_limit_bytes=LIMIT),
        cost_estimate=pl.CostEstimate(flops=int(flops), bytes_accessed=int(moved), transcendentals=0),
        input_output_aliases=alias or {},
    )(*args)


def cls_mlp(rows, grads, wide_w, down_w, vector, main=None):
    count, features = rows.shape
    hidden = wide_w.shape[1]
    tile = features
    whole = lambda shape: pl.BlockSpec(shape, lambda j: (0,) * len(shape))
    wide_block = pl.BlockSpec((features, tile), lambda j: (0, j))
    down_block = pl.BlockSpec((tile, features), lambda j: (j, 0))
    in_specs = [whole(rows.shape), whole(grads.shape), wide_block, down_block, whole(vector.shape)]
    args = [rows, grads, wide_w, down_w, vector]
    if main is None:
        out_shape = [jax.ShapeDtypeStruct(rows.shape, BF)] * 2
        out_specs = [whole(rows.shape)] * 2
    else:
        in_specs += [wide_block, down_block]
        args += list(main)
        out_shape = [
            jax.ShapeDtypeStruct(vector.shape, F32),
            jax.ShapeDtypeStruct(wide_w.shape, F32),
            jax.ShapeDtypeStruct(down_w.shape, F32),
        ]
        out_specs = [whole(vector.shape), wide_block, down_block]
    return pl.pallas_call(
        partial(cls_mlp_kernel, main is not None),
        grid=(hidden // tile,),
        in_specs=in_specs,
        out_specs=out_specs,
        out_shape=out_shape,
        scratch_shapes=[
            pltpu.VMEM((count, features), BF),
            pltpu.VMEM((count, features), F32),
            pltpu.VMEM((count, features), F32),
        ],
        compiler_params=pltpu.CompilerParams(vmem_limit_bytes=LIMIT),
    )(*args)


def cls_att_weights(rows, grads, layout, wide_w, vector):
    count, features = rows.shape
    block = min(count, 128)
    by_row = lambda width: pl.BlockSpec((block, width), lambda i: (i, 0))
    whole = lambda shape: pl.BlockSpec(shape, lambda i: (0,) * len(shape))
    return pl.pallas_call(
        partial(cls_att_bwd_kernel, True),
        grid=(count // block,),
        in_specs=[
            by_row(features), by_row(features), by_row(1), by_row(1),
            pl.BlockSpec((1, block), lambda i: (0, i)), whole(wide_w.shape), whole(vector.shape),
        ],
        out_specs=[whole(vector.shape), whole(wide_w.shape)],
        out_shape=[jax.ShapeDtypeStruct(vector.shape, F32), jax.ShapeDtypeStruct(wide_w.shape, F32)],
        compiler_params=pltpu.CompilerParams(vmem_limit_bytes=LIMIT),
    )(rows, grads, *layout, wide_w, vector)


def documents(counts):
    ends = jnp.cumsum(counts, -1)
    places = jnp.arange(SEGS, dtype=jnp.int32)
    doc = jnp.sum((places[:, None] >= ends[..., None, :]).astype(jnp.int32), -1)
    slots = jnp.arange(counts.shape[-1], dtype=jnp.int32)
    first = jnp.sum(jnp.where(doc[..., None] == slots, (ends - counts)[..., None, :], 0), -1)
    return doc, places - first


def row_layout(counts):
    doc, pos = documents(counts)
    packs = counts.shape[0]
    label = doc + jnp.arange(packs, dtype=jnp.int32)[:, None] * (counts.shape[1] + 1)
    return pos.reshape(-1, 1), label.reshape(-1, 1), label.reshape(1, -1)


def local(inputs, cotangent, wide, down, vectors, seg_counts):
    sections = lax.axis_size("section")
    section = lax.axis_index("section")
    core = lax.axis_index("dp") % 2
    rows, features = inputs.shape[1:]
    hidden = wide.shape[2]
    half, span = features // 2, hidden // 2
    wide_w, down_w, vector = wide[0], down[0], vectors[0]
    x, cot = inputs[0], cotangent[0]

    x_sib = swap_core(x)
    att_place = ring_position(ATT_RINGS, section, core)
    mlp_place = ring_position(MLP_RINGS, section, core)
    att_parts = [
        lax.dynamic_slice(wide_w, (0, k * features + core * half), (features, half)) for k in range(3)
    ] + [lax.dynamic_slice(wide_w, (core * half, 3 * features), (half, features))]
    wq, wk, wv, wo = broadcast(att_parts, ATT_RINGS, att_place)
    near = [swap_section(vector, bits) for bits in (1, 2, 3)]
    every_vector = jnp.stack([vector] + near)
    avec, mvec = pick(every_vector, section), pick(every_vector, section ^ 1)
    chunk = features
    mlp_parts = []
    for c in range(span // chunk):
        mlp_parts.append(lax.dynamic_slice(wide_w, (0, core * span + c * chunk), (features, chunk)))
        mlp_parts.append(lax.dynamic_slice(down_w, (core * span + c * chunk, 0), (chunk, features)))
    mlp_weights = broadcast(mlp_parts, MLP_RINGS, mlp_place)

    is_cls = (jnp.arange(rows) % SEG == 0)[:, None]
    plain_cot = jnp.where(is_cls, jnp.zeros_like(cot), cot)
    plain_sib = swap_core(plain_cot)
    plain_both = jnp.concatenate([plain_cot, plain_sib], 0)

    flops = 2 * 2 * rows * features * half * 4
    q, k, v, a, partial_out = call(
        att_fwd_kernel,
        [((2 * rows, half), BF)] * 4 + [((2 * rows, features), BF)],
        [x, x_sib, wq, wk, wv, wo, avec],
        [pltpu.VMEM((2 * rows, features), BF)],
        flops * 1.3,
        8 * 2**20,
    )
    partial_sib = swap_core(partial_out)
    h1, u1 = call(
        att_join_kernel,
        [((2 * rows, features), BF)] * 2,
        [x, x_sib, partial_out, partial_sib, avec, mvec],
        moved=8 * 2**20,
    )

    grid = lambda values: values.reshape(rows // SEG, SEG, features)
    count = sections * (rows // SEG)

    def collect(mine, owner):
        arrived = [
            permute(mine, lambda s, r: (owner, r), lambda s, r: s == owner ^ bits) for bits in (1, 2, 3)
        ]
        ordered = [None] * 4
        ordered[owner] = mine
        for bits, value in zip((1, 2, 3), arrived):
            ordered[owner ^ bits] = value
        return jnp.concatenate(ordered, 0)

    def spread(all_rows, owner):
        split = all_rows.reshape(sections, rows // SEG, features)
        arrived = [
            permute(split[owner ^ bits], lambda s, r: (owner ^ bits, r), lambda s, r: s == owner) for bits in (1, 2, 3)
        ]
        return jnp.where(section == owner, split[owner], arrived[0] + arrived[1] + arrived[2])

    def hop(all_rows, start, end):
        return permute(all_rows, lambda s, r: (end, r), lambda s, r: s == start)

    def on(column, run, outs):
        return lax.cond(section == column, lambda: list(run()), lambda: [jnp.zeros((count, features), BF)] * outs)

    counts_here = seg_counts[0]
    layout = row_layout(counts_here)
    cot_cls = collect(grid(cot)[:, 0], 3)
    cls1 = collect(grid(h1[:rows])[:, 0], 1)
    cls2, _ = on(1, lambda: cls_mlp(cls1, jnp.zeros_like(cls1), wide_w, down_w, vector), 2)
    cls2_at2 = hop(cls2, 1, 2)
    cls3 = on(2, lambda: call(cls_att_fwd_kernel, [((count, features), BF)], [cls2_at2, *layout, wide_w, vector]), 1)[0]
    cls3_at3 = hop(cls3, 2, 3)
    cls4, dcls3 = on(3, lambda: cls_mlp(cls3_at3, cot_cls, wide_w, down_w, vector), 2)
    dcls3_at2 = hop(dcls3, 3, 2)
    dcls2 = on(
        2,
        lambda: call(
            partial(cls_att_bwd_kernel, False), [((count, features), BF)], [cls2_at2, dcls3_at2, *layout, wide_w, vector]
        ),
        1,
    )[0]
    dcls2_at1 = hop(dcls2, 2, 1)
    _, dcls1 = on(1, lambda: cls_mlp(cls1, dcls2_at1, wide_w, down_w, vector), 2)
    dcls1_own = spread(dcls1, 1)
    cls4_own = spread(cls4, 3)

    flops = 2 * 2 * rows * features * chunk * 6
    mlp_grads = []
    out_acc = du_acc = None
    shapes = [((2 * rows, features), F32)] * 2 + [((4, 2 * features // 4, features), BF)]
    for c in range(span // chunk):
        args = [u1, plain_both, mlp_weights[2 * c], mlp_weights[2 * c + 1]]
        if c:
            args += [out_acc, du_acc]
        out_acc, du_acc, grad = call(
            partial(mlp_kernel, c == 0, 256),
            shapes,
            args,
            flops=flops,
            moved=12 * 2**20,
        )
        mlp_grads.append(grad)
    out_sib = swap_core(out_acc[rows:].astype(BF))
    du_sib = swap_core(du_acc[rows:].astype(BF))
    h2, dh1, mlp_small = call(
        mlp_done_kernel,
        [((rows, features), BF)] * 2 + [((8, features), F32)],
        [h1[:rows], plain_cot, out_acc[:rows], out_sib, du_acc[:rows], du_sib, mvec],
        moved=8 * 2**20,
    )
    place = lambda values, heads: lax.dynamic_update_slice(grid(values), heads[:, None], (0, 0, 0)).reshape(rows, features)
    layer_out = place(h2, cls4_own)
    dh1 = place(dh1, dcls1_own)

    dh1_sib = swap_core(dh1)
    att_grad, du0_own, du0_sib = call(
        att_bwd_kernel,
        [((4, features // 2, features), BF), ((rows, features), F32), ((rows, features), BF)],
        [x, x_sib, dh1, dh1_sib, q, k, v, a, wq, wk, wv, wo, avec],
        [pltpu.VMEM((2 * rows, features), BF)] + [pltpu.VMEM((2 * rows, half), BF)] * 4,
        2 * 2 * rows * features * half * 8 * 1.3,
        16 * 2**20,
    )
    input_grad, att_small = call(
        att_done_kernel,
        [((rows, features), BF), ((8, features), F32)],
        [x, dh1, du0_own, swap_core(du0_sib), avec],
        moved=6 * 2**20,
    )

    mlp_total = [reduce_pieces(grad, section, 1) for grad in mlp_grads]
    att_total = reduce_pieces(att_grad, section, 0)
    small = jnp.concatenate([att_small, mlp_small], 0)
    bits = 1
    while bits < lax.axis_size("dp"):
        small = small + swap_dp(small, bits)
        bits *= 2
    small = small + swap_section(small, 1)
    small = small + swap_section(small, 2)

    def both_cores(mine):
        other = swap_core(mine)
        return jnp.where(core == 0, mine, other), jnp.where(core == 0, other, mine)

    att_first, att_second = both_cores(att_total)
    mlp_halves = [both_cores(total) for total in mlp_total]

    mine_in = jnp.where(section == 1, cls1, jnp.where(section == 2, cls2_at2, cls3_at3))
    mine_grad = jnp.where(section == 1, dcls2_at1, jnp.where(section == 2, dcls3_at2, cot_cls))
    all_in = lax.all_gather(mine_in, "dp", axis=0, tiled=True)
    all_grad = lax.all_gather(mine_grad, "dp", axis=0, tiled=True)
    all_counts = lax.all_gather(counts_here, "dp", axis=0, tiled=True)
    all_layout = row_layout(all_counts)
    small_pad = jnp.zeros((vector.shape[0] - 3, features), F32)
    zero_down = lambda: jnp.zeros(down_w.shape, F32)

    def first_sums():
        (wide_sum,) = call(att_place_kernel, [(wide_w.shape, F32)], [att_first, att_second])
        return jnp.concatenate([small[0:3], small_pad], 0), wide_sum, zero_down()

    def second_sums():
        rows_w, rows_v = [], []
        for c in range(2):
            for halves in mlp_halves:
                piece = halves[c]
                rows_w.append(piece[:, : features // 4].reshape(features, chunk))
                rows_v.append(piece[:, features // 4 :].reshape(chunk, features))
        main = (jnp.concatenate(rows_w, 1), jnp.concatenate(rows_v, 0))
        cls_small, wide_sum, down_sum = cls_mlp(all_in, all_grad, wide_w, down_w, vector, main)
        return cls_small + jnp.concatenate([small[8:11], small_pad], 0), wide_sum, down_sum

    def third_sums():
        cls_small, wide_sum = cls_att_weights(all_in, all_grad, all_layout, wide_w, vector)
        return cls_small, wide_sum, zero_down()

    def fourth_sums():
        main = (jnp.zeros(wide_w.shape, BF), jnp.zeros(down_w.shape, BF))
        return tuple(cls_mlp(all_in, all_grad, wide_w, down_w, vector, main))

    vector_sum, wide_sum, down_sum = lax.switch(section, [first_sums, second_sums, third_sums, fourth_sums])
    return layer_out[None], input_grad[None], wide_sum[None], down_sum[None], vector_sum[None]


def solution(mesh):
    return jax.shard_map(
        local,
        mesh=mesh,
        in_specs=(
            P("section", "dp", None),
            P("section", "dp", None),
            P("section", None, None),
            P("section", None, None),
            P("section", None, None),
            P("dp", None, None),
        ),
        out_specs=(
            P("section", "dp", None),
            P("section", "dp", None),
            P("section", None, None),
            P("section", None, None),
            P("section", None, None),
        ),
        check_vma=False,
    )
```

time: 1430 us -> 572 us (0.40)
  waiting for transfers between devices: 688 us -> 166 us
  matrix products: 171 us -> 0 us
  local copies, waits for them, and re-layouts: 154 us -> 34.3 us
  loops' own time: 108 us -> 0.19 us
  Pallas kernels: 0 us -> 106 us
  other arithmetic: 128 us -> 35.3 us
  starting transfers between devices: 114 us -> 173 us
    psum x1 -> x0, waiting for transfers between devices: 376 us -> none  [local(): lax.psum((sum_wide, sum_down, sum_vector), 'dp')]
    dot_general x24 -> x0, matrix products: 171 us -> none  [product(): return jnp.dot(left_side, right_side, preferred_element_type=jnp.float32)]
    pallas_call x0 -> x10, Pallas kernels: none -> 106 us  [the longest x7 77.5 us: call(): pl.pallas_call(kernel, out_shape=[jax.ShapeDtypeStruct(*shape) for shape...]
    unnamed x7 -> x0, waiting for transfers between devices: 97.3 us -> none
    dynamic_update_slice x28 -> x0, other arithmetic: 81.5 us -> none  [put_slot(): lax.dynamic_update_index_in_dim(buffer, jnp.where(running, item, previous...]
    another operation x14 -> x6, loops' own time: 63.4 us -> 0.19 us  [the longest x1 0.11 us: local(): lax.switch(section, [first_sums, second_sums, third_sums, fourth_sums])]
    dynamic_slice x24 -> x4, local copies, waits for them, and re-layouts: 68.3 us -> 8.5 us  [the longest x1 3.23 us: local(): lax.dynamic_slice(down_w, (core * span + c * chunk, 0), (chunk, features))]
    ppermute x12 -> x82, starting transfers between devices: 114 us -> 173 us  [permute(): return lax.ppermute(shard, AXES, pairs)]
  transfers between devices with their start and end apart: 17 -> 82, of which waited for: 14 -> 18; matrix products, arithmetic and copies ran while one was open for 30% -> 9% of each run, Pallas kernels for 0% -> 16%
where the time goes in v1:
time: 572 us; the launch traced here: 563 us
  starting transfers between devices  173 us (30%)
  waiting for transfers between devices  166 us (29%)
  Pallas kernels  106 us (19%)
  blocking collectives  45.6 us (8%)
  other arithmetic  35.3 us (6%)
  local copies, waits for them, and re-layouts  34.3 us (6%)
    ppermute x82, starting transfers between devices, permute(): return lax.ppermute(shard, AXES, pairs)  173 us
    ppermute x82, waiting for transfers between devices, permute(): return lax.ppermute(shard, AXES, pairs)  166 us
    pallas_call x7, Pallas kernels, call(): pl.pallas_call(kernel, out_shape=[jax.ShapeDtypeStruct(*shape) for shape...  77.5 us
    pallas_call x3, Pallas kernels, cls_mlp(): pl.pallas_call(partial(cls_mlp_kernel, main is not None), grid=(hidden //...  28.6 us
    all_gather x1, blocking collectives, local(): all_grad = lax.all_gather(mine_grad, 'dp', axis=0, tiled=True)  15.8 us
    all_gather x1, blocking collectives, local(): all_in = lax.all_gather(mine_in, 'dp', axis=0, tiled=True)  15.4 us
    all_gather x1, blocking collectives, local(): all_counts = lax.all_gather(counts_here, 'dp', axis=0, tiled=True)  14.4 us
    select_n x8, other arithmetic, broadcast(): value = jnp.where(position == stage, hops[stage], value)  11.9 us
  transfers between devices with their start and end apart: 82, of which 18 were waited for; matrix products, arithmetic and copies ran while one was open for 9% of the time, Pallas kernels for 16%

profile of v1, /device:TPU:3, one launch (start us, length us, event | category | flops | bytes accessed | tf_op | source)
XLA Modules:
  0.0 563.0 jit_solution(1992794255622366148)
XLA Ops:
  13.9 15.1 %collective-permute-start.15 = (f32[7,768]{1,0:T(8,128)S(1)}, f32[7,768]{1,0:T(8,128)S(1)}, u32[]{:S(2)}, u32[]{:S(2)}) collective-permute-start(f32[7,768]{1,0:T(8,128)S(1)} %bitcast.149), channel_id=1, source_target_pairs={{0,24},{1,25},{2,26},{3,27},{4,28},{5,29},{6,30},{7,31},{8,16},{9,... | collective-permute-start | bytes 64520 | tf_op jit(solution)/shard_map/ppermute | solution.py:43
  29.0 7.2 %collective-permute-done.15 = f32[7,768]{1,0:T(8,128)S(1)} collective-permute-done((f32[7,768]{1,0:T(8,128)S(1)}, f32[7,768]{1,0:T(8,128)S(1)}, u32[]{:S(2)}, u32[]{:S(2)}) %collective-permute-start.15) | collective-permute-done | bytes 21536 | tf_op jit(solution)/shard_map/ppermute | solution.py:43
  36.2 6.6 %collective-permute-start.9 = (bf16[768,384]{1,0:T(8,128)(2,1)}, bf16[768,384]{1,0:T(8,128)(2,1)}, u32[]{:S(2)}, u32[]{:S(2)}) collective-permute-start(bf16[768,384]{1,0:T(8,128)(2,1)} %collective-permute-done.8), channel_id=1, source_target_pairs={{24,16},{25,9},{26,18},{27,11},{28,20},{29,13},{30,22},{31,15}} | collective-permute-start | bytes 1769480 | tf_op jit(solution)/shard_map/ppermute | solution.py:43
  43.7 3.2 dynamic-slice_bitcast_fusion
  46.9 3.6 collective-permute-start.27
  52.1 11.7 %collective-permute-start.6 = (bf16[768,384]{1,0:T(8,128)(2,1)}, bf16[768,384]{1,0:T(8,128)(2,1)}, u32[]{:S(2)}, u32[]{:S(2)}) collective-permute-start(bf16[768,384]{1,0:T(8,128)(2,1)} %collective-permute-done.5), channel_id=1, source_target_pairs={{24,16},{25,9},{26,18},{27,11},{28,20},{29,13},{30,22},{31,15}} | collective-permute-start | bytes 1769480 | tf_op jit(solution)/shard_map/ppermute | solution.py:43
  69.5 3.1 collective-permute-start.21
  75.5 4.0 collective-permute-done.3
  84.8 5.5 collective-permute-done.12
  94.2 14.7 %shard_map.101 = (bf16[1024,384]{1,0:T(8,128)(2,1)S(1)}, bf16[1024,384]{1,0:T(8,128)(2,1)S(1)}, bf16[1024,384]{1,0:T(8,128)(2,1)}, bf16[1024,384]{1,0:T(8,128)(2,1)}, bf16[1024,768]{1,0:T(8,128)(2,1)}) custom-call(bf16[512,768]{1,0:T(8,128)(2,1)} %bitcast.113, bf16[512,768]{1,0:T(8,128)(2,1)} %copy-done.3, bf16[768,384]{1,0:T(8,128)(2,1)S(1)} %select_select_fusion.7.wq, ...), custom_call_target="tpu_custom_call" | custom-call | flops 3140694784 | bytes 8388608 | tf_op jit(solution)/shard_map/pallas_call | solution.py:468
  113.6 5.6 %collective-permute-start.17 = (bf16[512,768]{1,0:T(8,128)(2,1)S(1)}, bf16[512,768]{1,0:T(8,128)(2,1)}, u32[]{:S(2)}, u32[]{:S(2)}) collective-permute-start(bf16[512,768]{1,0:T(8,128)(2,1)S(1)} %bitcast_select_fusion.b_ref), channel_id=1, source_target_pairs={{0,1},{1,0},{2,3},{3,2},{4,5},{5,4},{6,7},{7,6},{8,9},{9,8},{10,11... | collective-permute-start | bytes 2359304 | tf_op jit(solution)/shard_map/ppermute | solution.py:43
  126.4 5.4 shard_map.102
  133.2 3.0 collective-permute-done.34
  137.8 33.3 %collective-permute-done.33 = bf16[4,768]{1,0:T(4,128)(2,1)S(1)} collective-permute-done((bf16[4,768]{1,0:T(4,128)(2,1)S(1)}, bf16[4,768]{1,0:T(4,128)(2,1)S(1)}, u32[]{:S(2)}, u32[]{:S(2)}) %collective-permute-start.33) | collective-permute-done | bytes 6176 | tf_op jit(solution)/shard_map/ppermute | solution.py:43
  176.2 7.7 %conditional.6 = (bf16[16,768]{1,0:T(8,128)(2,1)S(1)}) conditional(s32[]{:T(128)} %convert_element_type.129, () %tuple.81, (bf16[16,768]{1,0:T(8,128)(2,1)S(1)}, bf16[768,3072]{1,0:T(8,128)(2,1)}, bf16[3072,768]{1,0:T(8,128)(2,1)}, f32[7,768]{1,0:T(8,128)S(1)}) %tuple.168), branch_computations={%region_0.1_spmd, %region_1.2_spmd} | conditional | bytes 24586 | solution.py:623
  176.2 7.6 %branch_1_fun.7 = (bf16[16,768]{1,0:T(8,128)(2,1)S(1)}, bf16[16,768]{1,0:T(8,128)(2,1)}) custom-call(bf16[16,768]{1,0:T(8,128)(2,1)S(1)} %get-tuple-element.232.h_ref, bf16[16,768]{1,0:T(8,128)(2,1)S(1)} %broadcast_6_b_ref.0.b_ref, bf16[768,3072]{1,0:T(8,128)(2,1)} %get-tuple-element.233.w_ref, bf16[3072,768]{1,0:T(8,128)(2,1)} %get-tuple-element.234.v_ref, ...), custom_call_target="tpu_custom_call" | custom-call | tf_op jit(solution)/shard_map/cond/branch_1_fun/pallas_call | solution.py:501
  193.6 12.0 %shard_map.103 = (f32[1024,768]{1,0:T(8,128)}, f32[1024,768]{1,0:T(8,128)}, bf16[4,384,768]{2,1,0:T(8,128)(2,1)}) custom-call(bf16[1024,768]{1,0:T(8,128)(2,1)S(1)} %copy-done.15, bf16[1024,768]{1,0:T(8,128)(2,1)} %pad_maximum_fusion.5.b_ref, bf16[768,768]{1,0:T(8,128)(2,1)S(1)} %select_select_fusion.1.w_ref, bf16[768,768]{1,0:T(8,128)(2,1)S(1)} %select_select_fusion.v_ref), custom_call_target="tpu_custom_call" | custom-call | flops 7247757312 | bytes 12582912 | tf_op jit(solution)/shard_map/pallas_call | solution.py:468
  207.0 14.2 %shard_map.104 = (f32[1024,768]{1,0:T(8,128)}, f32[1024,768]{1,0:T(8,128)}, bf16[4,384,768]{2,1,0:T(8,128)(2,1)}) custom-call(bf16[1024,768]{1,0:T(8,128)(2,1)S(1)} %copy-done.15, bf16[1024,768]{1,0:T(8,128)(2,1)} %pad_maximum_fusion.5.b_ref, bf16[768,768]{1,0:T(8,128)(2,1)S(1)} %select_select_fusion.3.w_ref, ...), custom_call_target="tpu_custom_call" | custom-call | flops 7247757312 | bytes 12582912 | tf_op jit(solution)/shard_map/pallas_call | solution.py:468
  229.6 15.7 %collective-permute-done.44 = bf16[16,768]{1,0:T(8,128)(2,1)S(1)} collective-permute-done((bf16[16,768]{1,0:T(8,128)(2,1)S(1)}, bf16[16,768]{1,0:T(8,128)(2,1)S(1)}, u32[]{:S(2)}, u32[]{:S(2)}) %collective-permute-start.44) | collective-permute-done | bytes 24608 | tf_op jit(solution)/shard_map/ppermute | solution.py:43
  245.3 7.6 %conditional.10 = (bf16[16,768]{1,0:T(8,128)(2,1)S(1)}) conditional(s32[]{:T(128)} %convert_element_type.129, () %tuple.85, (bf16[16,768]{1,0:T(8,128)(2,1)S(1)}, bf16[16,768]{1,0:T(8,128)(2,1)S(1)}, bf16[768,3072]{1,0:T(8,128)(2,1)}, bf16[3072,768]{1,0:T(8,128)(2,1)}, f32[7,768]{1,0:T(8,128)S(1)}) %tuple.172), branch_computations={%region_11.12_spmd, %region_12.13_spmd} | conditional | bytes 24586 | solution.py:623
  245.3 7.6 %branch_1_fun.11 = (bf16[16,768]{1,0:T(8,128)(2,1)}, bf16[16,768]{1,0:T(8,128)(2,1)S(1)}) custom-call(bf16[16,768]{1,0:T(8,128)(2,1)S(1)} %get-tuple-element.255.h_ref, bf16[16,768]{1,0:T(8,128)(2,1)S(1)} %get-tuple-element.256.b_ref, bf16[768,3072]{1,0:T(8,128)(2,1)} %get-tuple-element.257.w_ref, bf16[3072,768]{1,0:T(8,128)(2,1)} %get-tuple-element.258.v_ref, ...), custom_call_target="tpu_custom_call" | custom-call | tf_op jit(solution)/shard_map/cond/branch_1_fun/pallas_call | solution.py:501
  256.8 2.9 dynamic-slice_bitcast_fusion.6
  266.2 4.3 shard_map.105
  272.9 3.2 collective-permute-start.48
  277.6 4.6 collective-permute-start.64
  282.3 5.7 %collective-permute-start.66 = (bf16[384,768]{1,0:T(8,128)(2,1)S(1)}, bf16[384,768]{1,0:T(8,128)(2,1)S(1)}, u32[]{:S(2)}, u32[]{:S(2)}) collective-permute-start(bf16[384,768]{1,0:T(8,128)(2,1)S(1)} %get-tuple-element.474), channel_id=1, source_target_pairs={{0,24},{1,25},{2,26},{3,27},{4,28},{5,29},{6,30},{7,31},{8,16},{9,... | collective-permute-start | bytes 1769480 | tf_op jit(solution)/shard_map/ppermute | solution.py:43
  288.0 8.8 %collective-permute-start.65 = (bf16[384,768]{1,0:T(8,128)(2,1)S(1)}, bf16[384,768]{1,0:T(8,128)(2,1)S(1)}, u32[]{:S(2)}, u32[]{:S(2)}) collective-permute-start(bf16[384,768]{1,0:T(8,128)(2,1)S(1)} %get-tuple-element.475), channel_id=1, source_target_pairs={{0,16},{1,17},{2,18},{3,19},{4,20},{5,21},{6,22},{7,23},{8,24},{9,... | collective-permute-start | bytes 1769480 | tf_op jit(solution)/shard_map/ppermute | solution.py:43
  300.9 24.5 %shard_map.106 = (bf16[4,384,768]{2,1,0:T(8,128)(2,1)}, f32[512,768]{1,0:T(8,128)}, bf16[512,768]{1,0:T(8,128)(2,1)}) custom-call(bf16[512,768]{1,0:T(8,128)(2,1)S(1)} %bitcast.116, bf16[512,768]{1,0:T(8,128)(2,1)} %copy-done.3, bf16[512,768]{1,0:T(8,128)(2,1)} %bitcast.120, bf16[512,768]{1,0:T(8,128)(2,1)} %copy-done.34, bf16[1024,384]{1,0:T(8,128)(2,1)} %copy-done.16, ...), custom_call_target="tpu_custom_call" | custom-call | flops 6281389568 | bytes 16777216 | tf_op jit(solution)/shard_map/pallas_call | solution.py:468
  331.0 6.0 %collective-permute-start.67 = (bf16[384,768]{1,0:T(8,128)(2,1)S(1)}, bf16[384,768]{1,0:T(8,128)(2,1)S(1)}, u32[]{:S(2)}, u32[]{:S(2)}) collective-permute-start(bf16[384,768]{1,0:T(8,128)(2,1)S(1)} %fusion.5), channel_id=1, source_target_pairs={{0,2},{1,3},{2,0},{3,1},{4,6},{5,7},{6,4},{7,5},{8,10},{9,11},{10,... | collective-permute-start | bytes 1769480 | tf_op jit(solution)/shard_map/ppermute | solution.py:43
  341.2 13.6 %collective-permute-done.57 = bf16[384,768]{1,0:T(8,128)(2,1)S(1)} collective-permute-done((bf16[384,768]{1,0:T(8,128)(2,1)S(1)}, bf16[384,768]{1,0:T(8,128)(2,1)S(1)}, u32[]{:S(2)}, u32[]{:S(2)}) %collective-permute-start.57) | collective-permute-done | bytes 589856 | tf_op jit(solution)/shard_map/ppermute | solution.py:43
  356.5 7.7 %collective-permute-done.67 = bf16[384,768]{1,0:T(8,128)(2,1)S(1)} collective-permute-done((bf16[384,768]{1,0:T(8,128)(2,1)S(1)}, bf16[384,768]{1,0:T(8,128)(2,1)S(1)}, u32[]{:S(2)}, u32[]{:S(2)}) %collective-permute-start.67) | collective-permute-done | bytes 589856 | tf_op jit(solution)/shard_map/ppermute | solution.py:43
  364.4 4.0 collective-permute-start.68
  368.5 6.4 %collective-permute-start.80 = (bf16[384,768]{1,0:T(8,128)(2,1)S(1)}, bf16[384,768]{1,0:T(8,128)(2,1)S(1)}, u32[]{:S(2)}, u32[]{:S(2)}) collective-permute-start(bf16[384,768]{1,0:T(8,128)(2,1)S(1)} %add_convert_fusion), channel_id=1, source_target_pairs={{24,8},{25,9},{26,10},{27,11},{28,12},{29,13},{30,14},{31,15}} | collective-permute-start | bytes 1769480 | tf_op jit(solution)/shard_map/ppermute | solution.py:43
  374.9 9.6 %collective-permute-done.58 = bf16[384,768]{1,0:T(8,128)(2,1)S(1)} collective-permute-done((bf16[384,768]{1,0:T(8,128)(2,1)S(1)}, bf16[384,768]{1,0:T(8,128)(2,1)S(1)}, u32[]{:S(2)}, u32[]{:S(2)}) %collective-permute-start.58) | collective-permute-done | bytes 589856 | tf_op jit(solution)/shard_map/ppermute | solution.py:43
  384.7 24.5 %collective-permute-done.68 = bf16[384,768]{1,0:T(8,128)(2,1)S(1)} collective-permute-done((bf16[384,768]{1,0:T(8,128)(2,1)S(1)}, bf16[384,768]{1,0:T(8,128)(2,1)S(1)}, u32[]{:S(2)}, u32[]{:S(2)}) %collective-permute-start.68) | collective-permute-done | bytes 589856 | tf_op jit(solution)/shard_map/ppermute | solution.py:43
  413.2 6.1 %collective-permute-start.79 = (bf16[384,768]{1,0:T(8,128)(2,1)S(1)}, bf16[384,768]{1,0:T(8,128)(2,1)S(1)}, u32[]{:S(2)}, u32[]{:S(2)}) collective-permute-start(bf16[384,768]{1,0:T(8,128)(2,1)S(1)} %add_convert_fusion), channel_id=1, source_target_pairs={{16,8},{17,9},{18,10},{19,11},{20,12},{21,13},{22,14},{23,15}} | collective-permute-start | bytes 1769480 | tf_op jit(solution)/shard_map/ppermute | solution.py:43
  423.3 26.7 %collective-permute-done.71 = bf16[384,768]{1,0:T(8,128)(2,1)S(1)} collective-permute-done((bf16[384,768]{1,0:T(8,128)(2,1)S(1)}, bf16[384,768]{1,0:T(8,128)(2,1)S(1)}, u32[]{:S(2)}, u32[]{:S(2)}) %collective-permute-start.71) | collective-permute-done | bytes 589856 | tf_op jit(solution)/shard_map/ppermute | solution.py:43
  454.5 4.8 collective-permute-start.72
  461.1 5.7 %collective-permute-start.81 = (bf16[4,384,768]{2,1,0:T(8,128)(2,1)}, bf16[4,384,768]{2,1,0:T(8,128)(2,1)}, u32[]{:S(2)}, u32[]{:S(2)}) collective-permute-start(bf16[4,384,768]{2,1,0:T(8,128)(2,1)} %pad_maximum_fusion.4), channel_id=1, source_target_pairs={{0,1},{1,0},{2,3},{3,2},{4,5},{5,4},{6,7},{7,6},{8,9},{9,8},{10,11... | collective-permute-start | bytes 7077896 | tf_op jit(solution)/shard_map/ppermute | solution.py:43
  469.0 14.4 %all-gather = s32[1,32,4]{2,0,1:T(1,128)S(1)} all-gather(s32[1,4,4]{2,0,1:T(1,128)S(1)} %bitcast.187), channel_id=2, replica_groups=mesh['section'=4,'dp'=8] {'dp'}, dimensions={1}, use_global_device_ids=true | all-gather | bytes 576 | tf_op jit(solution)/shard_map/all_gather | solution.py:712
  493.1 15.4 %all_gather.9 = bf16[128,768]{1,0:T(8,128)(2,1)S(1)} all-gather(bf16[16,768]{1,0:T(8,128)(2,1)S(1)} %select_select_fusion.9), channel_id=1, replica_groups=mesh['section'=4,'dp'=8] {'dp'}, dimensions={0}, use_global_device_ids=true | all-gather | bytes 221184 | tf_op jit(solution)/shard_map/all_gather | solution.py:710
  508.9 5.0 collective-permute-done.52
  514.0 2.9 collective-permute-done.53
  519.2 15.8 %all_gather.10 = bf16[128,768]{1,0:T(8,128)(2,1)S(1)} all-gather(bf16[16,768]{1,0:T(8,128)(2,1)S(1)} %select_select_fusion.8), channel_id=1, replica_groups=mesh['section'=4,'dp'=8] {'dp'}, dimensions={0}, use_global_device_ids=true | all-gather | bytes 221184 | tf_op jit(solution)/shard_map/all_gather | solution.py:711
  536.6 25.4 %conditional.11 = (f32[1,768,3072]{2,1,0:T(8,128)}, f32[1,3072,768]{2,1,0:T(8,128)}, f32[1,7,768]{2,0,1:T(1,128)S(1)}) conditional(s32[]{:T(128)} %clamp.3, (f32[16,768]{1,0:T(8,128)S(1)}, pred[]{:T(512)}, bf16[4,384,768]{2,1,0:T(8,128)(2,1)}, bf16[4,384,768]{2,1,0:T(8,128)(2,1)}) %tuple.89, (pred[]{:T(512)}, ...), branch_computations={%region_14.15_spmd, %region_15.16_spmd, %region_16.19_spmd, %regio... | conditional | flops 42472704 | bytes 85048440 | solution.py:740
  536.6 4.1 broadcast_select_fusion.4
  544.1 2.7 pad_maximum_fusion.refs_0_
  548.6 13.3 %branch_1_fun.12 = (f32[7,768]{1,0:T(8,128)S(1)}, f32[768,3072]{1,0:T(8,128)}, f32[3072,768]{1,0:T(8,128)}) custom-call(bf16[128,768]{1,0:T(8,128)(2,1)S(1)} %get-tuple-element.265.h_ref, bf16[128,768]{1,0:T(8,128)(2,1)S(1)} %get-tuple-element.266.b_ref, bf16[768,3072]{1,0:T(8,128)(2,1)S(1)} %bitcast.133, bf16[3072,768]{1,0:T(8,128)(2,1)S(1)} %bitcast.140, ...), custom_call_target="tpu_custom_call" | custom-call | tf_op jit(solution)/shard_map/cond/branch_1_fun/pallas_call | solution.py:501
  (303 shorter events, 139.0 us)
Async XLA Ops:
  6.0 30.2 %collective-permute-start.8 = (bf16[768,384]{1,0:T(8,128)(2,1)S(1)}, bf16[768,384]{1,0:T(8,128)(2,1)}, u32[]{:S(2)}, u32[]{:S(2)}) collective-permute-start(bf16[768,384]{1,0:T(8,128)(2,1)S(1)} %collective-permute-done.7), channel_id=1, source_target_pairs={{8,24},{10,26},{12,28},{14,30},{17,25},{19,27},{21,29},{23,31}} | collective-permute-start | bytes 1769480 | tf_op jit(solution)/shard_map/ppermute | solution.py:43
  9.4 41.2 %collective-permute-start.10 = (bf16[384,768]{1,0:T(8,128)(2,1)}, bf16[384,768]{1,0:T(8,128)(2,1)}, u32[]{:S(2)}, u32[]{:S(2)}) collective-permute-start(bf16[384,768]{1,0:T(8,128)(2,1)} %dynamic-slice_bitcast_fusion.13), channel_id=1, source_target_pairs={{0,8},{1,17},{2,10},{3,19},{4,12},{5,21},{6,14},{7,23}} | collective-permute-start | bytes 1769480 | tf_op jit(solution)/shard_map/ppermute | solution.py:43
  10.9 41.2 %collective-permute-start.5 = (bf16[768,384]{1,0:T(8,128)(2,1)}, bf16[768,384]{1,0:T(8,128)(2,1)}, u32[]{:S(2)}, u32[]{:S(2)}) collective-permute-start(bf16[768,384]{1,0:T(8,128)(2,1)} %collective-permute-done.4), channel_id=1, source_target_pairs={{8,24},{10,26},{12,28},{14,30},{17,25},{19,27},{21,29},{23,31}} | collective-permute-start | bytes 1769480 | tf_op jit(solution)/shard_map/ppermute | solution.py:43
  12.4 51.4 %collective-permute-start.2 = (bf16[768,384]{1,0:T(8,128)(2,1)}, bf16[768,384]{1,0:T(8,128)(2,1)}, u32[]{:S(2)}, u32[]{:S(2)}) collective-permute-start(bf16[768,384]{1,0:T(8,128)(2,1)} %collective-permute-done.1), channel_id=1, source_target_pairs={{8,24},{10,26},{12,28},{14,30},{17,25},{19,27},{21,29},{23,31}} | collective-permute-start | bytes 1769480 | tf_op jit(solution)/shard_map/ppermute | solution.py:43
  13.9 22.3 %collective-permute-start.15 = (f32[7,768]{1,0:T(8,128)S(1)}, f32[7,768]{1,0:T(8,128)S(1)}, u32[]{:S(2)}, u32[]{:S(2)}) collective-permute-start(f32[7,768]{1,0:T(8,128)S(1)} %bitcast.149), channel_id=1, source_target_pairs={{0,24},{1,25},{2,26},{3,27},{4,28},{5,29},{6,30},{7,31},{8,16},{9,... | collective-permute-start | bytes 64520 | tf_op jit(solution)/shard_map/ppermute | solution.py:43
  36.2 30.7 %collective-permute-start.9 = (bf16[768,384]{1,0:T(8,128)(2,1)}, bf16[768,384]{1,0:T(8,128)(2,1)}, u32[]{:S(2)}, u32[]{:S(2)}) collective-permute-start(bf16[768,384]{1,0:T(8,128)(2,1)} %collective-permute-done.8), channel_id=1, source_target_pairs={{24,16},{25,9},{26,18},{27,11},{28,20},{29,13},{30,22},{31,15}} | collective-permute-start | bytes 1769480 | tf_op jit(solution)/shard_map/ppermute | solution.py:43
  46.9 36.5 %collective-permute-start.27 = (bf16[768,768]{1,0:T(8,128)(2,1)S(1)}, bf16[768,768]{1,0:T(8,128)(2,1)}, u32[]{:S(2)}, u32[]{:S(2)}) collective-permute-start(bf16[768,768]{1,0:T(8,128)(2,1)S(1)} %get-tuple-element.463), channel_id=1, source_target_pairs={{8,24},{9,1},{10,26},{11,3},{12,28},{13,5},{14,30},{15,7}} | collective-permute-start | bytes 3538952 | tf_op jit(solution)/shard_map/ppermute | solution.py:43
  52.1 21.1 %collective-permute-start.6 = (bf16[768,384]{1,0:T(8,128)(2,1)}, bf16[768,384]{1,0:T(8,128)(2,1)}, u32[]{:S(2)}, u32[]{:S(2)}) collective-permute-start(bf16[768,384]{1,0:T(8,128)(2,1)} %collective-permute-done.5), channel_id=1, source_target_pairs={{24,16},{25,9},{26,18},{27,11},{28,20},{29,13},{30,22},{31,15}} | collective-permute-start | bytes 1769480 | tf_op jit(solution)/shard_map/ppermute | solution.py:43
  66.9 26.5 %collective-permute-start = (bf16[512,768]{1,0:T(8,128)(2,1)S(1)}, bf16[512,768]{1,0:T(8,128)(2,1)S(1)}, u32[]{:S(2)}, u32[]{:S(2)}) collective-permute-start(bf16[512,768]{1,0:T(8,128)(2,1)S(1)} %bitcast.114), channel_id=1, source_target_pairs={{0,1},{1,0},{2,3},{3,2},{4,5},{5,4},{6,7},{7,6},{8,9},{9,8},{10,11... | collective-permute-start | bytes 2359304 | tf_op jit(solution)/shard_map/ppermute | solution.py:43
  69.5 40.4 %collective-permute-start.21 = (bf16[768,768]{1,0:T(8,128)(2,1)}, bf16[768,768]{1,0:T(8,128)(2,1)}, u32[]{:S(2)}, u32[]{:S(2)}) collective-permute-start(bf16[768,768]{1,0:T(8,128)(2,1)} %get-tuple-element.464), channel_id=1, source_target_pairs={{8,24},{9,1},{10,26},{11,3},{12,28},{13,5},{14,30},{15,7}} | collective-permute-start | bytes 3538952 | tf_op jit(solution)/shard_map/ppermute | solution.py:43
  73.1 38.5 %collective-permute-start.24 = (bf16[768,768]{1,0:T(8,128)(2,1)S(1)}, bf16[768,768]{1,0:T(8,128)(2,1)}, u32[]{:S(2)}, u32[]{:S(2)}) collective-permute-start(bf16[768,768]{1,0:T(8,128)(2,1)S(1)} %copy-done.22), channel_id=1, source_target_pairs={{8,24},{9,1},{10,26},{11,3},{12,28},{13,5},{14,30},{15,7}} | collective-permute-start | bytes 3538952 | tf_op jit(solution)/shard_map/ppermute | solution.py:43
  83.5 30.1 %collective-permute-start.18 = (bf16[768,768]{1,0:T(8,128)(2,1)}, bf16[768,768]{1,0:T(8,128)(2,1)S(1)}, u32[]{:S(2)}, u32[]{:S(2)}) collective-permute-start(bf16[768,768]{1,0:T(8,128)(2,1)} %get-tuple-element.466), channel_id=1, source_target_pairs={{8,24},{9,1},{10,26},{11,3},{12,28},{13,5},{14,30},{15,7}} | collective-permute-start | bytes 3538952 | tf_op jit(solution)/shard_map/ppermute | solution.py:43
  90.3 28.9 %collective-permute-start.28 = (bf16[768,768]{1,0:T(8,128)(2,1)}, bf16[768,768]{1,0:T(8,128)(2,1)}, u32[]{:S(2)}, u32[]{:S(2)}) collective-permute-start(bf16[768,768]{1,0:T(8,128)(2,1)} %collective-permute-done.27), channel_id=1, source_target_pairs={{1,17},{3,19},{5,21},{7,23},{24,16},{26,18},{28,20},{30,22}} | collective-permute-start | bytes 3538952 | tf_op jit(solution)/shard_map/ppermute | solution.py:43
  119.2 64.6 %collective-permute-start.29 = (bf16[768,768]{1,0:T(8,128)(2,1)}, bf16[768,768]{1,0:T(8,128)(2,1)}, u32[]{:S(2)}, u32[]{:S(2)}) collective-permute-start(bf16[768,768]{1,0:T(8,128)(2,1)} %collective-permute-done.28), channel_id=1, source_target_pairs={{16,0},{17,25},{18,2},{19,27},{20,4},{21,29},{22,6},{23,31}} | collective-permute-start | bytes 3538952 | tf_op jit(solution)/shard_map/ppermute | solution.py:43
  121.2 65.7 %collective-permute-start.19 = (bf16[768,768]{1,0:T(8,128)(2,1)}, bf16[768,768]{1,0:T(8,128)(2,1)}, u32[]{:S(2)}, u32[]{:S(2)}) collective-permute-start(bf16[768,768]{1,0:T(8,128)(2,1)} %copy-done.27), channel_id=1, source_target_pairs={{1,17},{3,19},{5,21},{7,23},{24,16},{26,18},{28,20},{30,22}} | collective-permute-start | bytes 3538952 | tf_op jit(solution)/shard_map/ppermute | solution.py:43
  122.9 64.9 %collective-permute-start.23 = (bf16[768,768]{1,0:T(8,128)(2,1)}, bf16[768,768]{1,0:T(8,128)(2,1)}, u32[]{:S(2)}, u32[]{:S(2)}) collective-permute-start(bf16[768,768]{1,0:T(8,128)(2,1)} %collective-permute-done.22), channel_id=1, source_target_pairs={{16,0},{17,25},{18,2},{19,27},{20,4},{21,29},{22,6},{23,31}} | collective-permute-start | bytes 3538952 | tf_op jit(solution)/shard_map/ppermute | solution.py:43
  124.7 65.7 %collective-permute-start.26 = (bf16[768,768]{1,0:T(8,128)(2,1)}, bf16[768,768]{1,0:T(8,128)(2,1)}, u32[]{:S(2)}, u32[]{:S(2)}) collective-permute-start(bf16[768,768]{1,0:T(8,128)(2,1)} %collective-permute-done.25), channel_id=1, source_target_pairs={{16,0},{17,25},{18,2},{19,27},{20,4},{21,29},{22,6},{23,31}} | collective-permute-start | bytes 3538952 | tf_op jit(solution)/shard_map/ppermute | solution.py:43
  136.2 34.9 %collective-permute-start.33 = (bf16[4,768]{1,0:T(4,128)(2,1)S(1)}, bf16[4,768]{1,0:T(4,128)(2,1)S(1)}, u32[]{:S(2)}, u32[]{:S(2)}) collective-permute-start(bf16[4,768]{1,0:T(4,128)(2,1)S(1)} %bitcast.179), channel_id=1, source_target_pairs={{16,8},{17,9},{18,10},{19,11},{20,12},{21,13},{22,14},{23,15}} | collective-permute-start | bytes 18440 | tf_op jit(solution)/shard_map/ppermute | solution.py:43
  175.5 51.3 %collective-permute-start.39 = (bf16[4,768]{1,0:T(4,128)(2,1)S(1)}, bf16[4,768]{1,0:T(4,128)(2,1)S(1)}, u32[]{:S(2)}, u32[]{:S(2)}) collective-permute-start(bf16[4,768]{1,0:T(4,128)(2,1)S(1)} %bitcast.173), channel_id=1, source_target_pairs={{16,24},{17,25},{18,26},{19,27},{20,28},{21,29},{22,30},{23,31}} | collective-permute-start | bytes 18440 | tf_op jit(solution)/shard_map/ppermute | solution.py:43
  183.8 43.7 %collective-permute-start.38 = (bf16[4,768]{1,0:T(4,128)(2,1)S(1)}, bf16[4,768]{1,0:T(4,128)(2,1)S(1)}, u32[]{:S(2)}, u32[]{:S(2)}) collective-permute-start(bf16[4,768]{1,0:T(4,128)(2,1)S(1)} %bitcast.174), channel_id=1, source_target_pairs={{8,24},{9,25},{10,26},{11,27},{12,28},{13,29},{14,30},{15,31}} | collective-permute-start | bytes 18440 | tf_op jit(solution)/shard_map/ppermute | solution.py:43
  187.0 40.5 %collective-permute-start.37 = (bf16[4,768]{1,0:T(4,128)(2,1)S(1)}, bf16[4,768]{1,0:T(4,128)(2,1)S(1)}, u32[]{:S(2)}, u32[]{:S(2)}) collective-permute-start(bf16[4,768]{1,0:T(4,128)(2,1)S(1)} %bitcast.175), channel_id=1, source_target_pairs={{0,24},{1,25},{2,26},{3,27},{4,28},{5,29},{6,30},{7,31}} | collective-permute-start | bytes 18440 | tf_op jit(solution)/shard_map/ppermute | solution.py:43
  190.4 35.6 %collective-permute-start.35 = (bf16[16,768]{1,0:T(8,128)(2,1)S(1)}, bf16[16,768]{1,0:T(8,128)(2,1)S(1)}, u32[]{:S(2)}, u32[]{:S(2)}) collective-permute-start(bf16[16,768]{1,0:T(8,128)(2,1)S(1)} %get-tuple-element.505), channel_id=1, source_target_pairs={{8,16},{9,17},{10,18},{11,19},{12,20},{13,21},{14,22},{15,23}} | collective-permute-start | bytes 73736 | tf_op jit(solution)/shard_map/ppermute | solution.py:43
  226.0 40.1 %collective-permute-start.31 = (bf16[512,768]{1,0:T(8,128)(2,1)}, bf16[512,768]{1,0:T(8,128)(2,1)S(1)}, u32[]{:S(2)}, u32[]{:S(2)}) collective-permute-start(bf16[512,768]{1,0:T(8,128)(2,1)} %slice.135), channel_id=1, source_target_pairs={{0,1},{1,0},{2,3},{3,2},{4,5},{5,4},{6,7},{7,6},{8,9},{9,8},{10,11... | collective-permute-start | bytes 2359304 | tf_op jit(solution)/shard_map/ppermute | solution.py:43
  226.0 40.1 %collective-permute-start.30 = (bf16[512,768]{1,0:T(8,128)(2,1)}, bf16[512,768]{1,0:T(8,128)(2,1)}, u32[]{:S(2)}, u32[]{:S(2)}) collective-permute-start(bf16[512,768]{1,0:T(8,128)(2,1)} %slice.136), channel_id=1, source_target_pairs={{0,1},{1,0},{2,3},{3,2},{4,5},{5,4},{6,7},{7,6},{8,9},{9,8},{10,11... | collective-permute-start | bytes 2359304 | tf_op jit(solution)/shard_map/ppermute | solution.py:43
  259.7 22.5 %collective-permute-start.73 = (bf16[384,768]{1,0:T(8,128)(2,1)}, bf16[384,768]{1,0:T(8,128)(2,1)}, u32[]{:S(2)}, u32[]{:S(2)}) collective-permute-start(bf16[384,768]{1,0:T(8,128)(2,1)} %get-tuple-element.470), channel_id=1, source_target_pairs={{0,8},{1,9},{2,10},{3,11},{4,12},{5,13},{6,14},{7,15},{8,0},{9,1},... | collective-permute-start | bytes 1769480 | tf_op jit(solution)/shard_map/ppermute | solution.py:43
  259.8 28.3 %collective-permute-start.75 = (bf16[384,768]{1,0:T(8,128)(2,1)}, bf16[384,768]{1,0:T(8,128)(2,1)}, u32[]{:S(2)}, u32[]{:S(2)}) collective-permute-start(bf16[384,768]{1,0:T(8,128)(2,1)} %get-tuple-element.471), channel_id=1, source_target_pairs={{0,24},{1,25},{2,26},{3,27},{4,28},{5,29},{6,30},{7,31},{8,16},{9,... | collective-permute-start | bytes 1769480 | tf_op jit(solution)/shard_map/ppermute | solution.py:43
  259.8 37.0 %collective-permute-start.74 = (bf16[384,768]{1,0:T(8,128)(2,1)}, bf16[384,768]{1,0:T(8,128)(2,1)}, u32[]{:S(2)}, u32[]{:S(2)}) collective-permute-start(bf16[384,768]{1,0:T(8,128)(2,1)} %get-tuple-element.472), channel_id=1, source_target_pairs={{0,16},{1,17},{2,18},{3,19},{4,20},{5,21},{6,22},{7,23},{8,24},{9,... | collective-permute-start | bytes 1769480 | tf_op jit(solution)/shard_map/ppermute | solution.py:43
  272.9 27.1 %collective-permute-start.48 = (bf16[512,768]{1,0:T(8,128)(2,1)}, bf16[512,768]{1,0:T(8,128)(2,1)S(1)}, u32[]{:S(2)}, u32[]{:S(2)}) collective-permute-start(bf16[512,768]{1,0:T(8,128)(2,1)} %bitcast.119), channel_id=1, source_target_pairs={{0,1},{1,0},{2,3},{3,2},{4,5},{5,4},{6,7},{7,6},{8,9},{9,8},{10,11... | collective-permute-start | bytes 2359304 | tf_op jit(solution)/shard_map/ppermute | solution.py:43
  277.6 49.6 %collective-permute-start.64 = (bf16[384,768]{1,0:T(8,128)(2,1)S(1)}, bf16[384,768]{1,0:T(8,128)(2,1)S(1)}, u32[]{:S(2)}, u32[]{:S(2)}) collective-permute-start(bf16[384,768]{1,0:T(8,128)(2,1)S(1)} %get-tuple-element.473), channel_id=1, source_target_pairs={{0,8},{1,9},{2,10},{3,11},{4,12},{5,13},{6,14},{7,15},{8,0},{9,1},... | collective-permute-start | bytes 1769480 | tf_op jit(solution)/shard_map/ppermute | solution.py:43
  282.3 47.1 %collective-permute-start.66 = (bf16[384,768]{1,0:T(8,128)(2,1)S(1)}, bf16[384,768]{1,0:T(8,128)(2,1)S(1)}, u32[]{:S(2)}, u32[]{:S(2)}) collective-permute-start(bf16[384,768]{1,0:T(8,128)(2,1)S(1)} %get-tuple-element.474), channel_id=1, source_target_pairs={{0,24},{1,25},{2,26},{3,27},{4,28},{5,29},{6,30},{7,31},{8,16},{9,... | collective-permute-start | bytes 1769480 | tf_op jit(solution)/shard_map/ppermute | solution.py:43
  288.0 41.6 %collective-permute-start.65 = (bf16[384,768]{1,0:T(8,128)(2,1)S(1)}, bf16[384,768]{1,0:T(8,128)(2,1)S(1)}, u32[]{:S(2)}, u32[]{:S(2)}) collective-permute-start(bf16[384,768]{1,0:T(8,128)(2,1)S(1)} %get-tuple-element.475), channel_id=1, source_target_pairs={{0,16},{1,17},{2,18},{3,19},{4,20},{5,21},{6,22},{7,23},{8,24},{9,... | collective-permute-start | bytes 1769480 | tf_op jit(solution)/shard_map/ppermute | solution.py:43
  298.8 38.3 %collective-permute-start.76 = (bf16[384,768]{1,0:T(8,128)(2,1)S(1)}, bf16[384,768]{1,0:T(8,128)(2,1)S(1)}, u32[]{:S(2)}, u32[]{:S(2)}) collective-permute-start(bf16[384,768]{1,0:T(8,128)(2,1)S(1)} %fusion.2), channel_id=1, source_target_pairs={{0,2},{1,3},{2,0},{3,1},{4,6},{5,7},{6,4},{7,5},{8,10},{9,11},{10,... | collective-permute-start | bytes 1769480 | tf_op jit(solution)/shard_map/ppermute | solution.py:43
  327.3 27.5 %collective-permute-start.57 = (bf16[384,768]{1,0:T(8,128)(2,1)S(1)}, bf16[384,768]{1,0:T(8,128)(2,1)S(1)}, u32[]{:S(2)}, u32[]{:S(2)}) collective-permute-start(bf16[384,768]{1,0:T(8,128)(2,1)S(1)} %get-tuple-element.477), channel_id=1, source_target_pairs={{0,24},{1,25},{2,26},{3,27},{4,28},{5,29},{6,30},{7,31},{8,16},{9,... | collective-permute-start | bytes 1769480 | tf_op jit(solution)/shard_map/ppermute | solution.py:43
  329.4 25.5 %collective-permute-start.56 = (bf16[384,768]{1,0:T(8,128)(2,1)S(1)}, bf16[384,768]{1,0:T(8,128)(2,1)S(1)}, u32[]{:S(2)}, u32[]{:S(2)}) collective-permute-start(bf16[384,768]{1,0:T(8,128)(2,1)S(1)} %get-tuple-element.478), channel_id=1, source_target_pairs={{0,16},{1,17},{2,18},{3,19},{4,20},{5,21},{6,22},{7,23},{8,24},{9,... | collective-permute-start | bytes 1769480 | tf_op jit(solution)/shard_map/ppermute | solution.py:43
  331.0 33.2 %collective-permute-start.67 = (bf16[384,768]{1,0:T(8,128)(2,1)S(1)}, bf16[384,768]{1,0:T(8,128)(2,1)S(1)}, u32[]{:S(2)}, u32[]{:S(2)}) collective-permute-start(bf16[384,768]{1,0:T(8,128)(2,1)S(1)} %fusion.5), channel_id=1, source_target_pairs={{0,2},{1,3},{2,0},{3,1},{4,6},{5,7},{6,4},{7,5},{8,10},{9,11},{10,... | collective-permute-start | bytes 1769480 | tf_op jit(solution)/shard_map/ppermute | solution.py:43
  337.2 31.2 %collective-permute-start.77 = (bf16[384,768]{1,0:T(8,128)(2,1)S(1)}, bf16[384,768]{1,0:T(8,128)(2,1)S(1)}, u32[]{:S(2)}, u32[]{:S(2)}) collective-permute-start(bf16[384,768]{1,0:T(8,128)(2,1)S(1)} %add_convert_fusion.1), channel_id=1, source_target_pairs={{0,4},{1,5},{2,6},{3,7},{4,0},{5,1},{6,2},{7,3},{8,12},{9,13},{10,... | collective-permute-start | bytes 1769480 | tf_op jit(solution)/shard_map/ppermute | solution.py:43
  356.2 28.3 %collective-permute-start.58 = (bf16[384,768]{1,0:T(8,128)(2,1)S(1)}, bf16[384,768]{1,0:T(8,128)(2,1)S(1)}, u32[]{:S(2)}, u32[]{:S(2)}) collective-permute-start(bf16[384,768]{1,0:T(8,128)(2,1)S(1)} %fusion.8), channel_id=1, source_target_pairs={{0,2},{1,3},{2,0},{3,1},{4,6},{5,7},{6,4},{7,5},{8,10},{9,11},{10,... | collective-permute-start | bytes 1769480 | tf_op jit(solution)/shard_map/ppermute | solution.py:43
  364.4 44.8 %collective-permute-start.68 = (bf16[384,768]{1,0:T(8,128)(2,1)S(1)}, bf16[384,768]{1,0:T(8,128)(2,1)S(1)}, u32[]{:S(2)}, u32[]{:S(2)}) collective-permute-start(bf16[384,768]{1,0:T(8,128)(2,1)S(1)} %add_convert_fusion.3), channel_id=1, source_target_pairs={{0,4},{1,5},{2,6},{3,7},{4,0},{5,1},{6,2},{7,3},{8,12},{9,13},{10,... | collective-permute-start | bytes 1769480 | tf_op jit(solution)/shard_map/ppermute | solution.py:43
  368.5 44.7 %collective-permute-start.80 = (bf16[384,768]{1,0:T(8,128)(2,1)S(1)}, bf16[384,768]{1,0:T(8,128)(2,1)S(1)}, u32[]{:S(2)}, u32[]{:S(2)}) collective-permute-start(bf16[384,768]{1,0:T(8,128)(2,1)S(1)} %add_convert_fusion), channel_id=1, source_target_pairs={{24,8},{25,9},{26,10},{27,11},{28,12},{29,13},{30,14},{31,15}} | collective-permute-start | bytes 1769480 | tf_op jit(solution)/shard_map/ppermute | solution.py:43
  384.6 37.2 %collective-permute-start.59 = (bf16[384,768]{1,0:T(8,128)(2,1)S(1)}, bf16[384,768]{1,0:T(8,128)(2,1)S(1)}, u32[]{:S(2)}, u32[]{:S(2)}) collective-permute-start(bf16[384,768]{1,0:T(8,128)(2,1)S(1)} %add_convert_fusion.5), channel_id=1, source_target_pairs={{0,4},{1,5},{2,6},{3,7},{4,0},{5,1},{6,2},{7,3},{8,12},{9,13},{10,... | collective-permute-start | bytes 1769480 | tf_op jit(solution)/shard_map/ppermute | solution.py:43
  409.3 40.7 %collective-permute-start.71 = (bf16[384,768]{1,0:T(8,128)(2,1)S(1)}, bf16[384,768]{1,0:T(8,128)(2,1)S(1)}, u32[]{:S(2)}, u32[]{:S(2)}) collective-permute-start(bf16[384,768]{1,0:T(8,128)(2,1)S(1)} %add_convert_fusion.2), channel_id=1, source_target_pairs={{24,8},{25,9},{26,10},{27,11},{28,12},{29,13},{30,14},{31,15}} | collective-permute-start | bytes 1769480 | tf_op jit(solution)/shard_map/ppermute | solution.py:43
  410.6 40.0 %collective-permute-start.70 = (bf16[384,768]{1,0:T(8,128)(2,1)S(1)}, bf16[384,768]{1,0:T(8,128)(2,1)S(1)}, u32[]{:S(2)}, u32[]{:S(2)}) collective-permute-start(bf16[384,768]{1,0:T(8,128)(2,1)S(1)} %add_convert_fusion.2), channel_id=1, source_target_pairs={{16,8},{17,9},{18,10},{19,11},{20,12},{21,13},{22,14},{23,15}} | collective-permute-start | bytes 1769480 | tf_op jit(solution)/shard_map/ppermute | solution.py:43
  411.9 39.5 %collective-permute-start.69 = (bf16[384,768]{1,0:T(8,128)(2,1)S(1)}, bf16[384,768]{1,0:T(8,128)(2,1)S(1)}, u32[]{:S(2)}, u32[]{:S(2)}) collective-permute-start(bf16[384,768]{1,0:T(8,128)(2,1)S(1)} %add_convert_fusion.2), channel_id=1, source_target_pairs={{0,8},{1,9},{2,10},{3,11},{4,12},{5,13},{6,14},{7,15}} | collective-permute-start | bytes 1769480 | tf_op jit(solution)/shard_map/ppermute | solution.py:43
  413.2 41.3 %collective-permute-start.79 = (bf16[384,768]{1,0:T(8,128)(2,1)S(1)}, bf16[384,768]{1,0:T(8,128)(2,1)S(1)}, u32[]{:S(2)}, u32[]{:S(2)}) collective-permute-start(bf16[384,768]{1,0:T(8,128)(2,1)S(1)} %add_convert_fusion), channel_id=1, source_target_pairs={{16,8},{17,9},{18,10},{19,11},{20,12},{21,13},{22,14},{23,15}} | collective-permute-start | bytes 1769480 | tf_op jit(solution)/shard_map/ppermute | solution.py:43
  421.8 37.5 %collective-permute-start.78 = (bf16[384,768]{1,0:T(8,128)(2,1)S(1)}, bf16[384,768]{1,0:T(8,128)(2,1)S(1)}, u32[]{:S(2)}, u32[]{:S(2)}) collective-permute-start(bf16[384,768]{1,0:T(8,128)(2,1)S(1)} %add_convert_fusion), channel_id=1, source_target_pairs={{0,8},{1,9},{2,10},{3,11},{4,12},{5,13},{6,14},{7,15}} | collective-permute-start | bytes 1769480 | tf_op jit(solution)/shard_map/ppermute | solution.py:43
  454.5 82.0 %collective-permute-start.72 = (bf16[4,384,768]{2,1,0:T(8,128)(2,1)}, bf16[4,384,768]{2,1,0:T(8,128)(2,1)}, u32[]{:S(2)}, u32[]{:S(2)}) collective-permute-start(bf16[4,384,768]{2,1,0:T(8,128)(2,1)} %pad_maximum_fusion.3), channel_id=1, source_target_pairs={{0,1},{1,0},{2,3},{3,2},{4,5},{5,4},{6,7},{7,6},{8,9},{9,8},{10,11... | collective-permute-start | bytes 7077896 | tf_op jit(solution)/shard_map/ppermute | solution.py:43
  461.1 75.5 %collective-permute-start.81 = (bf16[4,384,768]{2,1,0:T(8,128)(2,1)}, bf16[4,384,768]{2,1,0:T(8,128)(2,1)}, u32[]{:S(2)}, u32[]{:S(2)}) collective-permute-start(bf16[4,384,768]{2,1,0:T(8,128)(2,1)} %pad_maximum_fusion.4), channel_id=1, source_target_pairs={{0,1},{1,0},{2,3},{3,2},{4,5},{5,4},{6,7},{7,6},{8,9},{9,8},{10,11... | collective-permute-start | bytes 7077896 | tf_op jit(solution)/shard_map/ppermute | solution.py:43
  468.5 68.1 %collective-permute-start.63 = (bf16[4,384,768]{2,1,0:T(8,128)(2,1)}, bf16[4,384,768]{2,1,0:T(8,128)(2,1)}, u32[]{:S(2)}, u32[]{:S(2)}) collective-permute-start(bf16[4,384,768]{2,1,0:T(8,128)(2,1)} %pad_maximum_fusion.2), channel_id=1, source_target_pairs={{0,1},{1,0},{2,3},{3,2},{4,5},{5,4},{6,7},{7,6},{8,9},{9,8},{10,11... | collective-permute-start | bytes 7077896 | tf_op jit(solution)/shard_map/ppermute | solution.py:43
  (71 other events, 771.7 us)
